TPU v7x, 512 devices: a whole 4x8x8 slice. The times are simulated.
512 devices in a mesh: ctx: 64 (over z, x, core), head: 8 (over y).
Axes of the slice: x: 4, y: 8, z: 8, core: 2. Of those that a mesh axis runs over, the one named last changes fastest.
Arguments:
- latents: bfloat16 [512, 2048], P('ctx'), may hold values from -40 to 40
- context: bfloat16 [16384, 2048], P('ctx', 'head'), may hold values from -40 to 40
- lengths: int32 [512], replicated, may hold values from 1 to 16384, as said below
- w_query: bfloat16 [2048, 2048], P(None, 'head'), may hold values from -1 to 1
- w_key: bfloat16 [2048, 2048], P(None, 'head'), may hold values from -1 to 1
- w_value: bfloat16 [2048, 2048], P(None, 'head'), may hold values from -0.125 to 0.125
- w_out: bfloat16 [2048, 2048], P('head'), may hold values from -0.25 to 0.25
Outputs:
- mixed: bfloat16 [512, 2048], P('ctx', 'head')
Inputs may be any that keep to these rules, and one draw needn't show every extreme that they name: `lengths`: some latent sees all 16384 positions and some latent only the first.
All inputs are finite; a program needn't handle non-finite values.
Results may differ from a plain program's by a relative error of at most 0.0095.
The roundings to bfloat16 on the way count: a program that leaves them out, or rounds other values in their place, can miss the bound.
Values may be sent and summed in bfloat16 or wider, within the bound.
No kernel may reach another device: no remote copies, remote signals or barrier semaphores. Data moves between devices by JAX's collectives and lax.ppermute only.
A program may use at most 128 MiB of HBM per device.

v0:
```python
import jax
import jax.numpy as jnp
from jax import lax
from jax.sharding import PartitionSpec as P

HD = 128


def combined_all(part, axis, combine):
    gathered = jax.tree.map(lambda a: lax.all_gather(a, axis), part)

    def take(source):
        return jax.tree.map(lambda a: lax.dynamic_index_in_dim(a, source, 0, False), gathered)

    return lax.fori_loop(
        1, lax.axis_size(axis), lambda source, state: combine(state, take(source)), take(0)
    )


def slab_attention(queries, lens, keys, values, positions):
    scores = jnp.einsum("bhd,chd->hbc", queries, keys, preferred_element_type=jnp.float32)
    visible = positions[None, :] < lens[:, None]
    scores = jnp.where(visible[None], scores, -jnp.inf)
    top = jnp.maximum(jnp.max(scores, axis=2), -1e30)
    probs = jnp.exp(scores - top[:, :, None]).astype(jnp.bfloat16)
    total = jnp.sum(probs.astype(jnp.float32), axis=2)
    out = jnp.einsum("hbc,chd->bhd", probs, values, preferred_element_type=jnp.float32)
    return (top, total, out.reshape(out.shape[0], -1))


def combine_pair(first, second):
    top_a, total_a, out_a = first
    top_b, total_b, out_b = second
    heads = top_a.shape[0]
    top = jnp.maximum(top_a, top_b)
    scale_a = jnp.exp(top_a - top)
    scale_b = jnp.exp(top_b - top)
    total = scale_a * total_a + scale_b * total_b
    rows = out_a.shape[0]
    out = (
        out_a.reshape(rows, heads, -1) * scale_a.T[:, :, None]
        + out_b.reshape(rows, heads, -1) * scale_b.T[:, :, None]
    )
    return (top, total, out.reshape(rows, -1))


def on_device(latents, context, lengths, w_query, w_key, w_value, w_out):
    lat_dev = latents.shape[0]
    groups = lax.axis_size("ctx")
    latent_count = lat_dev * groups
    width_heads = w_query.shape[1]
    heads_dev = width_heads // HD
    qscale = 1.0 / HD**0.5
    local_q = (jnp.dot(latents, w_query, preferred_element_type=jnp.float32) * qscale).astype(
        jnp.bfloat16
    )
    queries = lax.all_gather(local_q, "ctx", axis=0, tiled=True)
    ctx_dev = context.shape[0]
    piece = lax.all_gather(context, "head", axis=1, tiled=True)
    key_sum = jnp.dot(piece, w_key, preferred_element_type=jnp.float32)
    value_sum = jnp.dot(piece, w_value, preferred_element_type=jnp.float32)
    keys = key_sum.astype(jnp.bfloat16).reshape(ctx_dev, heads_dev, HD)
    values = value_sum.astype(jnp.bfloat16).reshape(ctx_dev, heads_dev, HD)
    positions = lax.axis_index("ctx") * ctx_dev + jnp.arange(ctx_dev, dtype=jnp.int32)
    block = min(512, latent_count)
    blocks = latent_count // block
    query_blocks = queries.reshape(blocks, block, heads_dev, HD)
    length_blocks = lengths.reshape(blocks, block)

    def attend(item):
        return slab_attention(item[0], item[1], keys, values, positions)

    top, total, out = lax.map(attend, (query_blocks, length_blocks))
    top = top.transpose(1, 0, 2).reshape(heads_dev, latent_count)
    total = total.transpose(1, 0, 2).reshape(heads_dev, latent_count)
    out = out.reshape(latent_count, width_heads)
    merged_top, merged_total, merged_out = combined_all((top, total, out), "ctx", combine_pair)
    first_row = lax.axis_index("ctx") * lat_dev
    own_total = lax.dynamic_slice_in_dim(merged_total, first_row, lat_dev, 1)
    own_out = lax.dynamic_slice_in_dim(merged_out, first_row, lat_dev, 0)
    attended = (
        (own_out.reshape(lat_dev, heads_dev, HD) / own_total.T[:, :, None])
        .reshape(lat_dev, width_heads)
        .astype(jnp.bfloat16)
    )
    projected = jnp.dot(attended, w_out, preferred_element_type=jnp.float32)
    summed = lax.psum_scatter(projected, "head", scatter_dimension=1, tiled=True)
    first_col = lax.axis_index("head") * summed.shape[1]
    residual = lax.dynamic_slice_in_dim(latents, first_col, summed.shape[1], 1).astype(jnp.float32)
    return (residual + summed).astype(jnp.bfloat16)


def solution(mesh):
    in_specs = (
        P("ctx", None),
        P("ctx", "head"),
        P(),
        P(None, "head"),
        P(None, "head"),
        P(None, "head"),
        P("head", None),
    )
    out_specs = P("ctx", "head")
    return jax.shard_map(
        on_device, mesh=mesh, in_specs=in_specs, out_specs=out_specs, check_vma=False
    )
```

profile of v0, /device:TPU:6, one launch (start us, length us, event | category | flops | bytes accessed | tf_op | source)
XLA Modules:
  0.0 445.4 jit_solution(9177257818859600651)
XLA Ops:
  7.3 1.5 fusion.5
  8.8 49.9 %all_gather.15 = bf16[512,256]{1,0:T(8,128)(2,1)S(1)} all-gather(bf16[8,256]{1,0:T(8,128)(2,1)S(1)} %fusion.5), channel_id=1, replica_groups=mesh['ctx'=64,'head'=8] {'ctx'}, dimensions={0}, use_global_device_ids=true | all-gather | bytes 266240 | tf_op jit(solution)/shard_map/all_gather | solution.py:57
  59.6 1.7 convolution_convert_fusion.1
  61.7 2.1 convolution_convert_fusion
  65.3 41.8 %all-gather.3 = f32[64,2,512]{2,1,0:T(2,128)S(1)} all-gather(f32[1,2,512]{2,1,0:T(2,128)S(1)} %bitcast.90), channel_id=3, replica_groups=mesh['ctx'=64,'head'=8] {'ctx'}, dimensions={0}, use_global_device_ids=true | all-gather | bytes 266240 | tf_op jit(solution)/shard_map/all_gather | solution.py:10
  107.1 43.5 %all-gather.2 = f32[64,2,512]{2,1,0:T(2,128)S(1)} all-gather(f32[1,2,512]{2,1,0:T(2,128)S(1)} %get-tuple-element.230), channel_id=2, replica_groups=mesh['ctx'=64,'head'=8] {'ctx'}, dimensions={0}, use_global_device_ids=true | all-gather | bytes 266240 | tf_op jit(solution)/shard_map/all_gather | solution.py:10
  150.6 58.5 %all-gather.9.cloned.1.call-done = f32[64,512,256]{2,1,0:T(8,128)} async-done(((f32[1,512,256]{2,1,0:T(8,128)}), f32[64,512,256]{2,1,0:T(8,128)}) %all-gather.9.cloned.1.call-update) | async-done | bytes 33554448 | tf_op jit(solution)/shard_map/all_gather | solution.py:10
  210.2 188.0 %while.12 = (s32[]{:T(128)}, f32[2,512]{1,0:T(2,128)S(1)}, f32[2,512]{1,0:T(2,128)S(1)}, f32[512,256]{1,0:T(8,128)S(1)}, f32[64,2,512]{2,1,0:T(2,128)S(1)}, /*in...) while((s32[]{:T(128)}, f32[2,512]{1,0:T(2,128)S(1)}, ...), condition=%wide.region_3.4_spmd, body=%wide.region_2.3_spmd.sunk | while | flops 400389 | bytes 3747987 | solution.py:15
  211.8 1.4 fusion.31
  217.8 1.4 fusion.31
  226.7 1.4 fusion.31
  232.7 1.4 fusion.31
  238.7 1.4 fusion.31
  244.6 1.4 fusion.31
  250.6 1.4 fusion.31
  256.6 1.4 fusion.31
  262.5 1.4 fusion.31
  268.5 1.4 fusion.31
  274.5 1.4 fusion.31
  283.4 1.4 fusion.31
  289.4 1.4 fusion.31
  295.4 1.4 fusion.31
  398.3 2.1 fusion.10
  400.5 37.2 %reduce-scatter.2.cloned.1.call-done = f32[8,256]{1,0:T(8,128)} async-done(((f32[8,2048]{1,0:T(8,128)}), f32[8,256]{1,0:T(8,128)}) %reduce-scatter.2.cloned.1.call-update) | async-done | bytes 8208 | tf_op jit(solution)/shard_map/reduce_scatter | solution.py:87
  (511 shorter events, 171.1 us)
Async XLA Ops:
  6.5 53.0 %copy-start = (bf16[2048,256]{1,0:T(8,128)(2,1)S(1)}, bf16[2048,256]{1,0:T(8,128)(2,1)}, u32[]{:S(2)}) copy-start(bf16[2048,256]{1,0:T(8,128)(2,1)} %param.13) | copy-start | bytes 3145732
  6.5 53.0 %all-gather.7.cloned.1.call-start = ((), (), s32[]{:S(2)}) async-start(), calls=%async_computation.1 | async-start | bytes 1179648 | tf_op jit(solution)/shard_map/all_gather | solution.py:59
  7.3 201.8 %all-gather.9.cloned.1.call-start = ((), (), s32[]{:S(2)}) async-start(), calls=%async_computation.2 | async-start | bytes 34078720 | tf_op jit(solution)/shard_map/all_gather | solution.py:10
  65.1 372.5 %reduce-scatter.2.cloned.1.call-start = ((), (), s32[]{:S(2)}) async-start(), calls=%async_computation.3 | async-start | bytes 73728 | tf_op jit(solution)/shard_map/reduce_scatter | solution.py:87
Sparse Core Ops, SparseCore 0:
  9.4 46.6 all-gather.6
  65.3 143.8 all-gather.8
  400.6 37.0 reduce-scatter.1
where the time goes:
time: 449 us; the launch traced here: 445 us
  blocking collectives  135 us (30%)
  local copies, waits for them, and re-layouts  97.1 us (22%)
  waiting for transfers between devices  96.5 us (21%)
  other arithmetic  91.8 us (20%)
  between operations  13.2 us (3%)
  matrix products  8.14 us (2%)
    add x63, other arithmetic, combine_pair(): out_a.reshape(rows, heads, -1) * scale_a.T[:, :, None]  86.7 us
    all_gather x2, blocking collectives, combined_all(): gathered = jax.tree.map(lambda a: lax.all_gather(a, axis), part)  85.2 us
    all_gather x1, waiting for transfers between devices, combined_all(): gathered = jax.tree.map(lambda a: lax.all_gather(a, axis), part)  58.5 us
    all_gather x1, blocking collectives, on_device(): queries = lax.all_gather(local_q, 'ctx', axis=0, tiled=True)  49.9 us
    mul x63, local copies, waits for them, and re-layouts, combine_pair(): out_a.reshape(rows, heads, -1) * scale_a.T[:, :, None]  38.1 us
    mul x63, local copies, waits for them, and re-layouts, combine_pair(): out_b.reshape(rows, heads, -1) * scale_b.T[:, :, None]  38.1 us
    reduce_scatter x1, waiting for transfers between devices, on_device(): lax.psum_scatter(projected, 'head', scatter_dimension=1, tiled=True)  37.2 us
    transpose x63, local copies, waits for them, and re-layouts, combine_pair(): scale_b.T[:, :, None]  9.45 us
  transfers between devices with their start and end apart: 3, of which 2 were waited for; matrix products, arithmetic and copies ran while one was open for 1% of the time, Pallas kernels for 0%

commit v1 on v0

v1 whole, which is shorter than its diff:
```python
import jax
import jax.numpy as jnp
from jax import lax
from jax.sharding import PartitionSpec as P

HD = 128
PAD = 128
BF = jnp.bfloat16
F32 = jnp.float32


def split3(a):
    hi = lax.reduce_precision(a, 8, 7)
    rest = a - hi
    mid = lax.reduce_precision(rest, 8, 7)
    return hi.astype(BF), mid.astype(BF), (rest - mid).astype(BF)


def join3(hi, mid, lo):
    return hi.astype(F32) + (mid.astype(F32) + lo.astype(F32))


def on_device(latents, context, lengths, w_query, w_key, w_value, w_out):
    lat_dev = latents.shape[0]
    groups = lax.axis_size("ctx")
    heads_axis = lax.axis_size("head")
    latent_count = lat_dev * groups
    width = w_query.shape[1]
    heads = width // HD
    ctx_dev = context.shape[0]
    qscale = 1.0 / HD**0.5

    piece = lax.all_gather(context, "head", axis=1, tiled=True)

    local_q = (jnp.dot(latents, w_query, preferred_element_type=F32) * qscale).astype(BF)
    queries = lax.all_to_all(
        jnp.broadcast_to(local_q[None], (groups, lat_dev, width)), "ctx", 0, 0
    )
    queries = queries.reshape(latent_count, heads, HD)

    keys = jnp.dot(piece, w_key, preferred_element_type=F32).astype(BF).reshape(ctx_dev, heads, HD)
    values = jnp.dot(piece, w_value, preferred_element_type=F32).astype(BF).reshape(ctx_dev, heads, HD)
    positions = lax.axis_index("ctx") * ctx_dev + jnp.arange(ctx_dev, dtype=jnp.int32)
    scores = jnp.einsum("bhd,chd->hbc", queries, keys, preferred_element_type=F32)
    visible = positions[None, :] < lengths[:, None]
    scores = jnp.where(visible[None], scores, -jnp.inf)
    top = jnp.maximum(jnp.max(scores, axis=2), -1e30)
    probs = jnp.exp(scores - top[:, :, None]).astype(BF)
    total = jnp.sum(probs.astype(F32), axis=2)
    out = jnp.einsum("hbc,chd->bhd", probs, values, preferred_element_type=F32)

    cols = [p[h][:, None] for h in range(heads) for p in split3(top) + split3(total)]
    meta = jnp.concatenate(cols, axis=1)
    meta = jnp.pad(meta, ((0, 0), (0, PAD - meta.shape[1])))
    packed = jnp.concatenate([out.reshape(latent_count, width).astype(BF), meta], axis=1)
    got = lax.all_to_all(packed.reshape(groups, lat_dev, width + PAD), "ctx", 0, 0)

    parts = []
    for h in range(heads):
        m = got[:, :, width + 6 * h : width + 6 * h + 6]
        t = join3(m[..., 0:1], m[..., 1:2], m[..., 2:3])
        n = join3(m[..., 3:4], m[..., 4:5], m[..., 5:6])
        scale = jnp.exp(t - jnp.max(t, axis=0, keepdims=True))
        o = jnp.sum(scale * got[:, :, h * HD : (h + 1) * HD].astype(F32), axis=0)
        parts.append((o / jnp.sum(scale * n, axis=0)).astype(BF))
    attended = jnp.concatenate(parts, axis=1)

    projected = jnp.dot(attended, w_out, preferred_element_type=F32)
    cols_dev = projected.shape[1] // heads_axis
    shares = projected.reshape(lat_dev, heads_axis, cols_dev).transpose(1, 0, 2)
    summed = jnp.sum(lax.all_to_all(shares, "head", 0, 0), axis=0)
    first_col = lax.axis_index("head") * cols_dev
    residual = lax.dynamic_slice_in_dim(latents, first_col, cols_dev, 1).astype(F32)
    return (residual + summed).astype(BF)


def solution(mesh):
    in_specs = (
        P("ctx", None),
        P("ctx", "head"),
        P(),
        P(None, "head"),
        P(None, "head"),
        P(None, "head"),
        P("head", None),
    )
    return jax.shard_map(
        on_device, mesh=mesh, in_specs=in_specs, out_specs=P("ctx", "head"), check_vma=False
    )
```

time: 449 us -> 115 us (0.26)
  blocking collectives: 135 us -> 25.5 us
  other arithmetic: 91.8 us -> 2.51 us
  local copies, waits for them, and re-layouts: 97.1 us -> 8.56 us
  waiting for transfers between devices: 96.5 us -> 40.8 us
  starting transfers between devices: 0.08 us -> 18.7 us
    all_gather x3 -> x0, blocking collectives: 135 us -> none  [the longest x2 85.2 us: combined_all(): gathered = jax.tree.map(lambda a: lax.all_gather(a, axis), part)]
    add x63 -> x0, other arithmetic: 86.7 us -> none  [combine_pair(): out_a.reshape(rows, heads, -1) * scale_a.T[:, :, None]]
    mul x126 -> x2, local copies, waits for them, and re-layouts: 76.2 us -> 0.17 us  [on_device(): o = jnp.sum(scale * got[:, :, h * HD:(h + 1) * HD].astype(F32), axis=0)]
    all_gather x1 -> x0, waiting for transfers between devices: 58.5 us -> none  [combined_all(): gathered = jax.tree.map(lambda a: lax.all_gather(a, axis), part)]
    reduce_scatter x1 -> x0, waiting for transfers between devices: 37.2 us -> none  [on_device(): lax.psum_scatter(projected, 'head', scatter_dimension=1, tiled=True)]
    all_to_all x0 -> x1, blocking collectives: none -> 25.5 us  [on_device(): lax.all_to_all(packed.reshape(groups, lat_dev, width + PAD), 'ctx', 0, 0)]
    all_gather x1, waiting for transfers between devices: 0.02 us -> 20.6 us  [on_device(): piece = lax.all_gather(context, 'head', axis=1, tiled=True)]
    all_to_all x0 -> x2, waiting for transfers between devices: none -> 19.5 us  [the longest x1 11.1 us: on_device(): lax.all_to_all(jnp.broadcast_to(local_q[None], (groups, lat_dev, width)),...]
  transfers between devices with their start and end apart: 3 -> 3, of which waited for: 2 -> 3; matrix products, arithmetic and copies ran while one was open for 1% -> 2% of each run, Pallas kernels for 0% -> 0%
where the time goes in v1:
time: 115 us
  waiting for transfers between devices  40.8 us (35%)
  blocking collectives  25.5 us (22%)
  starting transfers between devices  18.7 us (16%)
  between operations  13.6 us (12%)
  local copies, waits for them, and re-layouts  8.56 us (7%)
  matrix products  5.32 us (5%)
  other arithmetic  2.51 us (2%)
    all_to_all x1, blocking collectives, on_device(): lax.all_to_all(packed.reshape(groups, lat_dev, width + PAD), 'ctx', 0, 0)  25.5 us
    all_gather x1, waiting for transfers between devices, on_device(): piece = lax.all_gather(context, 'head', axis=1, tiled=True)  20.6 us
    all_to_all x1, starting transfers between devices, on_device(): lax.all_to_all(jnp.broadcast_to(local_q[None], (groups, lat_dev, width)),...  13.8 us
    all_to_all x1, waiting for transfers between devices, on_device(): lax.all_to_all(jnp.broadcast_to(local_q[None], (groups, lat_dev, width)),...  11.1 us
    all_to_all x1, waiting for transfers between devices, on_device(): summed = jnp.sum(lax.all_to_all(shares, 'head', 0, 0), axis=0)  8.38 us
    unnamed x29, local copies, waits for them, and re-layouts  6.15 us
    all_to_all x1, starting transfers between devices, on_device(): summed = jnp.sum(lax.all_to_all(shares, 'head', 0, 0), axis=0)  4.89 us
  transfers between devices with their start and end apart: 3, of which 3 were waited for; matrix products, arithmetic and copies ran while one was open for 2% of the time, Pallas kernels for 0%

profile of v1, /device:TPU:6, one launch (start us, length us, event | category | flops | bytes accessed | tf_op | source)
XLA Modules:
  0.0 114.9 jit_solution(16747509446890371764)
XLA Ops:
  6.5 0.7 all-gather.2.cloned.1.call-update
  7.4 1.5 %fusion = bf16[8,256]{1,0:T(8,128)(2,1)S(1)} fusion(bf16[8,2048]{1,0:T(8,128)(2,1)S(1)} %copy-done.4, bf16[2048,256]{1,0:T(8,128)(2,1)} %param.10), kind=kOutput, calls=%fused_computation.5 | convolution fusion | flops 8392704 | bytes 1085440 | tf_op jit(solution)/shard_map/dot_general | solution.py:35
  8.9 0.7 broadcast_in_dim.15
  9.6 13.8 %all-to-all-start = ((bf16[64,8,256]{2,1,0:T(8,128)(2,1)}), bf16[64,8,256]{2,1,0:T(8,128)(2,1)S(1)}, u32[]{:S(2)}, u32[]{:S(2)}) async-start(bf16[64,8,256]{2,1,0:T(8,128)(2,1)} %broadcast_in_dim.15), calls=%async_computation | async-start | bytes 524288 | tf_op jit(solution)/shard_map/all_to_all | solution.py:36
  23.4 0.7 copy-done.6
  24.3 11.1 %all-to-all-done = bf16[64,8,256]{2,1,0:T(8,128)(2,1)S(1)} async-done(((bf16[64,8,256]{2,1,0:T(8,128)(2,1)}), bf16[64,8,256]{2,1,0:T(8,128)(2,1)S(1)}, u32[]{:S(2)}, u32[]{:S(2)}) %all-to-all-start) | async-done | bytes 262176 | tf_op jit(solution)/shard_map/all_to_all | solution.py:36
  35.4 20.6 %all-gather.2.cloned.1.call-done = bf16[256,2048]{1,0:T(8,128)(2,1)} async-done(((bf16[256,256]{1,0:T(8,128)(2,1)}), bf16[256,2048]{1,0:T(8,128)(2,1)}) %all-gather.2.cloned.1.call-update) | async-done | bytes 1048592 | tf_op jit(solution)/shard_map/all_gather | solution.py:33
  56.0 1.7 %convolution_convert_fusion.1 = bf16[256,256]{0,1:T(8,128)(2,1)S(1)} fusion(bf16[256,2048]{1,0:T(8,128)(2,1)} %all-gather.2.cloned.1.call-done, bf16[2048,256]{1,0:T(8,128)(2,1)S(1)} %copy-done), kind=kOutput, calls=%fused_computation.2 | convolution fusion | flops 268500992 | bytes 2228224 | tf_op jit(solution)/shard_map/dot_general | solution.py:41
  57.8 0.4 fusion.17
  58.4 0.6 copy-done.1
  59.0 0.3 copy-done.2
  59.3 0.5 convolution_convert_fusion.2
  59.9 0.3 convolution_convert_fusion
  60.7 25.5 %all_to_all.15 = bf16[64,8,384]{2,1,0:T(8,128)(2,1)S(1)} all-to-all(bf16[64,8,384]{2,1,0:T(8,128)(2,1)S(1)} %fusion.3), channel_id=1, replica_groups=mesh['ctx'=64,'head'=8] {'ctx'}, dimensions={0} | all-to-all | bytes 786432 | tf_op jit(solution)/shard_map/all_to_all | solution.py:56
  86.1 1.1 fusion.16
  87.2 0.7 copy.80
  88.3 1.1 copy.83
  90.8 0.2 multiply_reduce_fusion.2
  91.2 0.6 copy-done.5
  92.0 0.2 multiply_reduce_fusion.1
  92.6 0.9 fusion.7
  93.5 4.9 %all-to-all-start.2 = ((f32[8,8,256]{2,1,0:T(8,128)}), f32[8,8,256]{2,1,0:T(8,128)S(1)}, u32[]{:S(2)}, u32[]{:S(2)}) async-start(f32[8,8,256]{2,1,0:T(8,128)} %bitcast.20), calls=%async_computation.2 | async-start | bytes 131072 | tf_op jit(solution)/shard_map/all_to_all | solution.py:71
  98.4 8.4 %all-to-all-done.2 = f32[8,8,256]{2,1,0:T(8,128)S(1)} async-done(((f32[8,8,256]{2,1,0:T(8,128)}), f32[8,8,256]{2,1,0:T(8,128)S(1)}, u32[]{:S(2)}, u32[]{:S(2)}) %all-to-all-start.2) | async-done | bytes 65568 | tf_op jit(solution)/shard_map/all_to_all | solution.py:71
  106.8 1.3 %add_convert_fusion = bf16[8,256]{1,0:T(8,128)(2,1)} fusion(f32[8,256]{1,0:T(8,128)S(1)} %reduce_sum.59, bf16[8,2048]{1,0:T(8,128)(2,1)} %param.7, s32[]{:T(128)S(6)} %select_n.7), kind=kLoop, calls=%fused_computation.18 | loop fusion | flops 6144 | bytes 16388 | tf_op jit(solution)/shard_map/convert_element_type | solution.py:74
  (46 shorter events, 3.5 us)
Async XLA Ops:
  6.5 49.5 %copy-start = (bf16[2048,256]{1,0:T(8,128)(2,1)S(1)}, bf16[2048,256]{1,0:T(8,128)(2,1)}, u32[]{:S(2)}) copy-start(bf16[2048,256]{1,0:T(8,128)(2,1)} %param.11) | copy-start | bytes 3145732
  6.5 0.8 copy-start.4
  6.5 49.5 %all-gather.2.cloned.1.call-start = ((), (), s32[]{:S(2)}) async-start(), calls=%async_computation.3 | async-start | bytes 1179648 | tf_op jit(solution)/shard_map/all_gather | solution.py:33
  9.6 25.8 %all-to-all-start = ((bf16[64,8,256]{2,1,0:T(8,128)(2,1)}), bf16[64,8,256]{2,1,0:T(8,128)(2,1)S(1)}, u32[]{:S(2)}, u32[]{:S(2)}) async-start(bf16[64,8,256]{2,1,0:T(8,128)(2,1)} %broadcast_in_dim.15), calls=%async_computation | async-start | bytes 524288 | tf_op jit(solution)/shard_map/all_to_all | solution.py:36
  23.4 0.7 copy-start.6
  57.8 1.2 %copy-start.1 = (bf16[256,2048]{1,0:T(8,128)(2,1)S(1)}, bf16[256,2048]{1,0:T(8,128)(2,1)}, u32[]{:S(2)}) copy-start(bf16[256,2048]{1,0:T(8,128)(2,1)} %all-gather.2.cloned.1.call-done) | copy-start | bytes 3145732
  57.8 1.5 %copy-start.2 = (bf16[2048,256]{1,0:T(8,128)(2,1)S(1)}, bf16[2048,256]{1,0:T(8,128)(2,1)}, u32[]{:S(2)}) copy-start(bf16[2048,256]{1,0:T(8,128)(2,1)} %param.12) | copy-start | bytes 3145732
  88.3 4.4 %copy-start.3 = (bf16[256,2048]{1,0:T(8,128)(2,1)S(1)}, bf16[256,2048]{1,0:T(8,128)(2,1)}, u32[]{:S(2)}) copy-start(bf16[256,2048]{1,0:T(8,128)(2,1)} %param.13) | copy-start | bytes 3145732
  91.1 0.7 copy-start.5
  93.5 13.3 %all-to-all-start.2 = ((f32[8,8,256]{2,1,0:T(8,128)}), f32[8,8,256]{2,1,0:T(8,128)S(1)}, u32[]{:S(2)}, u32[]{:S(2)}) async-start(f32[8,8,256]{2,1,0:T(8,128)} %bitcast.20), calls=%async_computation.2 | async-start | bytes 131072 | tf_op jit(solution)/shard_map/all_to_all | solution.py:71
Sparse Core Ops, SparseCore 0:
  9.4 46.6 all-gather.1

commit v2 on v1

v2 whole, which is shorter than its diff:
```python
import jax
import jax.numpy as jnp
from jax import lax
from jax.experimental import pallas as pl
from jax.experimental.pallas import tpu as pltpu
from jax.sharding import PartitionSpec as P

HD = 128
META = 128
CORES = 2
BF = jnp.bfloat16
F32 = jnp.float32
LIMIT = 40 * 1024 * 1024


def split3(a):
    hi = a.astype(BF).astype(F32)
    rest = a - hi
    mid = rest.astype(BF).astype(F32)
    return [hi, mid, (rest - mid).astype(BF).astype(F32)]


def pack_meta(tops, totals):
    rows = tops[0].shape[0]
    lane = lax.broadcasted_iota(jnp.int32, (rows, META), 1)
    meta = jnp.zeros((rows, META), F32)
    column = 0
    for top, total in zip(tops, totals):
        for part in split3(top) + split3(total):
            meta = jnp.where(lane == column, part, meta)
            column += 1
    return meta.astype(BF)


def read_meta(meta, head):
    m = meta.astype(F32)
    part = [m[..., 6 * head + i : 6 * head + i + 1] for i in range(6)]
    return part[0] + (part[1] + part[2]), part[3] + (part[4] + part[5])


def attend_kernel(place, x, wk, wv, q, lens, keep, send):
    core, base = place[0], place[1]
    heads = wk.shape[1] // HD
    rows, width = q.shape[1], q.shape[2]
    positions = x.shape[1]
    feats = jnp.concatenate([x[f] for f in range(x.shape[0])], axis=1)
    k = jnp.dot(feats, wk[...], preferred_element_type=F32).astype(BF)
    v = jnp.dot(feats, wv[...], preferred_element_type=F32).astype(BF)
    ones = jnp.ones((positions, HD), BF)
    pos = base + lax.broadcasted_iota(jnp.int32, (rows, positions), 1)
    for half, ref in ((1 - core, send), (core, keep)):
        visible = pos < lens[half]
        qh = q[half]
        tops, totals = [], []
        for h in range(heads):
            cols = slice(h * HD, (h + 1) * HD)
            s = lax.dot_general(
                qh[:, cols], k[:, cols], (((1,), (1,)), ((), ())), preferred_element_type=F32
            )
            s = jnp.where(visible, s, -jnp.inf)
            top = jnp.maximum(jnp.max(s, axis=1, keepdims=True), -1e30)
            probs = jnp.exp(s - top).astype(BF)
            both = jnp.dot(
                probs, jnp.concatenate([v[:, cols], ones], axis=1), preferred_element_type=F32
            )
            ref[:, cols] = both[:, :HD].astype(ref.dtype)
            tops.append(top)
            totals.append(both[:, HD : HD + 1])
        ref[:, width:] = pack_meta(tops, totals).astype(ref.dtype)


def pair_kernel(place, keep, got, out):
    other = 1 - place[0]
    width = keep.shape[1] - META
    theirs = got[other]
    tops, totals = [], []
    for h in range(width // HD):
        cols = slice(h * HD, (h + 1) * HD)
        top_a, total_a = read_meta(keep[:, width:], h)
        top_b, total_b = read_meta(theirs[:, width:], h)
        top = jnp.maximum(top_a, top_b)
        scale_a, scale_b = jnp.exp(top_a - top), jnp.exp(top_b - top)
        out[:, cols] = (scale_a * keep[:, cols] + scale_b * theirs[:, cols].astype(F32)).astype(BF)
        tops.append(top)
        totals.append(scale_a * total_a + scale_b * total_b)
    out[:, width:] = pack_meta(tops, totals)


def project_kernel(got, w_out, out):
    width = w_out.shape[0]
    parts = []
    for h in range(width // HD):
        top, total = read_meta(got[:, :, width:], h)
        scale = jnp.exp(top - jnp.max(top, axis=0, keepdims=True))
        o = jnp.sum(scale * got[:, :, h * HD : (h + 1) * HD].astype(F32), axis=0)
        parts.append((o / jnp.sum(scale * total, axis=0)).astype(BF))
    projected = jnp.dot(jnp.concatenate(parts, axis=1), w_out[...], preferred_element_type=F32)
    cols = out.shape[2]
    for d in range(out.shape[0]):
        out[d] = projected[:, d * cols : (d + 1) * cols]


def call(kernel, shapes, n_in, smem_first):
    vmem = pl.BlockSpec(memory_space=pltpu.VMEM)
    specs = [vmem] * n_in
    if smem_first:
        specs[0] = pl.BlockSpec(memory_space=pltpu.SMEM)
    return pl.pallas_call(
        kernel,
        out_shape=shapes,
        in_specs=specs,
        out_specs=jax.tree.map(lambda _: vmem, shapes),
        compiler_params=pltpu.CompilerParams(vmem_limit_bytes=LIMIT),
    )


def on_device(latents, context, lengths, w_query, w_key, w_value, w_out):
    lat_dev = latents.shape[0]
    groups = lax.axis_size("ctx")
    heads_axis = lax.axis_size("head")
    width = w_query.shape[1]
    ctx_dev = context.shape[0]
    chips = groups // CORES
    half = chips * lat_dev
    qscale = 1.0 / HD**0.5
    me = lax.axis_index("ctx")
    place = jnp.stack([me % CORES, me * ctx_dev]).astype(jnp.int32)
    same_core = [[c + CORES * g for g in range(chips)] for c in range(CORES)]
    core_pairs = [[CORES * g + c for c in range(CORES)] for g in range(chips)]

    x = lax.all_to_all(
        jnp.broadcast_to(context[None], (heads_axis,) + context.shape), "head", 0, 0
    )

    q = (jnp.dot(latents, w_query, preferred_element_type=F32) * qscale).astype(BF)
    bit = CORES
    while bit < groups:
        pairs = [[i, i | bit] for i in range(groups) if not i & bit]
        q = lax.all_gather(q, "ctx", axis=0, tiled=True, axis_index_groups=pairs)
        bit *= 2
    q = lax.all_gather(q, "ctx", axis=0, axis_index_groups=core_pairs)
    lens = lengths.reshape(chips, CORES, lat_dev).transpose(1, 0, 2).reshape(CORES, half, 1)

    keep, send = call(
        attend_kernel,
        [
            jax.ShapeDtypeStruct((half, width + META), F32),
            jax.ShapeDtypeStruct((half, width + META), BF),
        ],
        6,
        True,
    )(place, x, w_key, w_value, q, lens)
    got = lax.all_gather(send, "ctx", axis=0, axis_index_groups=core_pairs)
    paired = call(pair_kernel, jax.ShapeDtypeStruct((half, width + META), BF), 3, True)(
        place, keep, got
    )
    got = lax.all_to_all(
        paired.reshape(chips, lat_dev, width + META), "ctx", 0, 0, axis_index_groups=same_core
    )
    cols_dev = w_out.shape[1] // heads_axis
    shares = call(
        project_kernel, jax.ShapeDtypeStruct((heads_axis, lat_dev, cols_dev), F32), 2, False
    )(got, w_out)
    summed = jnp.sum(lax.all_to_all(shares, "head", 0, 0), axis=0)
    first_col = lax.axis_index("head") * cols_dev
    residual = lax.dynamic_slice_in_dim(latents, first_col, cols_dev, 1).astype(F32)
    return (residual + summed).astype(BF)


def solution(mesh):
    in_specs = (
        P("ctx", None),
        P("ctx", "head"),
        P(),
        P(None, "head"),
        P(None, "head"),
        P(None, "head"),
        P("head", None),
    )
    return jax.shard_map(
        on_device, mesh=mesh, in_specs=in_specs, out_specs=P("ctx", "head"), check_vma=False
    )
```

time: 115 us -> 92.8 us (0.81)
  waiting for transfers between devices: 40.8 us -> 8.38 us
  blocking collectives: 25.5 us -> 57.4 us
  between operations: 13.6 us -> 0.08 us
  matrix products: 5.32 us -> 0.24 us
  Pallas kernels: 0 us -> 5.05 us
  starting transfers between devices: 18.7 us -> 14.4 us
  local copies, waits for them, and re-layouts: 8.56 us -> 5.7 us
  other arithmetic: 2.51 us -> 0.69 us
    all_gather x0 -> x7, blocking collectives: none -> 36.6 us  [the longest x5 32.2 us: on_device(): q = lax.all_gather(q, 'ctx', axis=0, tiled=True, axis_index_groups=pairs)]
    all_gather x1 -> x0, waiting for transfers between devices: 20.6 us -> none  [on_device(): piece = lax.all_gather(context, 'head', axis=1, tiled=True)]
    all_to_all x1, waiting for transfers between devices: 11.1 us -> 0.01 us  [on_device(): lax.all_to_all(jnp.broadcast_to(context[None], (heads_axis,) + context.sh...]
    all_to_all x1, starting transfers between devices: 13.8 us -> 7.1 us  [on_device(): lax.all_to_all(jnp.broadcast_to(context[None], (heads_axis,) + context.sh...]
    pallas_call x0 -> x3, Pallas kernels: none -> 5.05 us  [the longest x1 2.37 us: on_device(): call(attend_kernel, [jax.ShapeDtypeStruct((half, width + META), F32), jax...]
    all_to_all x1, blocking collectives: 25.5 us -> 20.9 us  [on_device(): lax.all_to_all(paired.reshape(chips, lat_dev, width + META), 'ctx', 0, 0,...]
    dot_general x5 -> x0, matrix products: 3.85 us -> none  [the longest x1 1.74 us: on_device(): jnp.dot(piece, w_key, preferred_element_type=F32).astype(BF)]
    unnamed x29 -> x14, local copies, waits for them, and re-layouts: 6.15 us -> 3.45 us
  transfers between devices with their start and end apart: 3 -> 2, of which waited for: 3 -> 1; matrix products, arithmetic and copies ran while one was open for 2% -> 1% of each run, Pallas kernels for 0% -> 0%
where the time goes in v2:
time: 92.8 us; the launch traced here: 92 us
  blocking collectives  57.4 us (62%)
  starting transfers between devices  14.4 us (16%)
  waiting for transfers between devices  8.38 us (9%)
  local copies, waits for them, and re-layouts  5.7 us (6%)
  Pallas kernels  5.05 us (5%)
    all_gather x5, blocking collectives, on_device(): q = lax.all_gather(q, 'ctx', axis=0, tiled=True, axis_index_groups=pairs)  32.2 us
    all_to_all x1, blocking collectives, on_device(): lax.all_to_all(paired.reshape(chips, lat_dev, width + META), 'ctx', 0, 0,...  20.9 us
    all_to_all x1, waiting for transfers between devices, on_device(): summed = jnp.sum(lax.all_to_all(shares, 'head', 0, 0), axis=0)  8.38 us
    all_to_all x1, starting transfers between devices, on_device(): summed = jnp.sum(lax.all_to_all(shares, 'head', 0, 0), axis=0)  7.33 us
    all_to_all x1, starting transfers between devices, on_device(): lax.all_to_all(jnp.broadcast_to(context[None], (heads_axis,) + context.sh...  7.1 us
    unnamed x14, local copies, waits for them, and re-layouts  3.45 us
    pallas_call x1, Pallas kernels, on_device(): call(attend_kernel, [jax.ShapeDtypeStruct((half, width + META), F32), jax...  2.37 us
    all_gather x1, blocking collectives, on_device(): got = lax.all_gather(send, 'ctx', axis=0, axis_index_groups=core_pairs)  2.22 us
  transfers between devices with their start and end apart: 2, of which 1 were waited for; matrix products, arithmetic and copies ran while one was open for 1% of the time, Pallas kernels for 0%

profile of v2, /device:TPU:6, one launch (start us, length us, event | category | flops | bytes accessed | tf_op | source)
XLA Modules:
  0.0 92.0 jit_solution(14318529918126980260)
XLA Ops:
  0.0 2.0 %broadcast_in_dim.2 = bf16[8,256,256]{2,1,0:T(8,128)(2,1)} broadcast(bf16[256,256]{1,0:T(8,128)(2,1)} %param.8), dimensions={1,2} | broadcast | bytes 1179648 | tf_op jit(solution)/shard_map/broadcast_in_dim | solution.py:132
  2.0 7.1 %all-to-all-start = ((bf16[8,256,256]{2,1,0:T(8,128)(2,1)}), bf16[8,256,256]{2,1,0:T(8,128)(2,1)S(1)}, u32[]{:S(2)}, u32[]{:S(2)}) async-start(bf16[8,256,256]{2,1,0:T(8,128)(2,1)} %broadcast_in_dim.2), calls=%async_computation | async-start | bytes 2097152 | tf_op jit(solution)/shard_map/all_to_all | solution.py:131
  9.1 0.7 copy-done.6
  9.8 0.1 reshape.10
  10.0 0.1 reshape.15.lens
  10.1 0.6 copy-done.5
  10.7 0.2 fusion
  10.9 4.3 %all_gather.27 = bf16[16,256]{1,0:T(8,128)(2,1)S(1)} all-gather(bf16[8,256]{1,0:T(8,128)(2,1)S(1)} %fusion), channel_id=1, replica_groups={{0,16},{8,24},{32,48},{40,56},{64,80},{72,88},{96,112},{104,120},{128,1..., dimensions={0}, use_global_device_ids=true | all-gather | bytes 12288 | tf_op jit(solution)/shard_map/all_gather | solution.py:139
  15.3 5.9 %all_gather.28 = bf16[32,256]{1,0:T(8,128)(2,1)S(1)} all-gather(bf16[16,256]{1,0:T(8,128)(2,1)S(1)} %all_gather.27), channel_id=1, replica_groups={{0,32},{8,40},{16,48},{24,56},{64,96},{72,104},{80,112},{88,120},{128,1..., dimensions={0}, use_global_device_ids=true | all-gather | bytes 24576 | tf_op jit(solution)/shard_map/all_gather | solution.py:139
  21.1 4.7 %all_gather.29 = bf16[64,256]{1,0:T(8,128)(2,1)S(1)} all-gather(bf16[32,256]{1,0:T(8,128)(2,1)S(1)} %all_gather.28), channel_id=1, replica_groups={{0,64},{8,72},{16,80},{24,88},{32,96},{40,104},{48,112},{56,120},{128,1..., dimensions={0}, use_global_device_ids=true | all-gather | bytes 49152 | tf_op jit(solution)/shard_map/all_gather | solution.py:139
  25.8 6.7 %all_gather.30 = bf16[128,256]{1,0:T(8,128)(2,1)S(1)} all-gather(bf16[64,256]{1,0:T(8,128)(2,1)S(1)} %all_gather.29), channel_id=1, replica_groups={{0,128},{8,136},{16,144},{24,152},{32,160},{40,168},{48,176},{56,184},{..., dimensions={0}, use_global_device_ids=true | all-gather | bytes 98304 | tf_op jit(solution)/shard_map/all_gather | solution.py:139
  32.6 10.6 %all_gather.31 = bf16[256,256]{1,0:T(8,128)(2,1)S(1)} all-gather(bf16[128,256]{1,0:T(8,128)(2,1)S(1)} %all_gather.30), channel_id=1, replica_groups={{0,256},{8,264},{16,272},{24,280},{32,288},{40,296},{48,304},{56,312},{..., dimensions={0}, use_global_device_ids=true | all-gather | bytes 196608 | tf_op jit(solution)/shard_map/all_gather | solution.py:139
  43.2 2.1 %all-gather = bf16[512,256]{1,0:T(8,128)(2,1)} all-gather(bf16[256,256]{1,0:T(8,128)(2,1)S(1)} %all_gather.31), channel_id=2, replica_groups={{0,8},{16,24},{32,40},{48,56},{64,72},{80,88},{96,104},{112,120},{128,1..., dimensions={0}, use_global_device_ids=true | all-gather | bytes 393216 | tf_op jit(solution)/shard_map/all_gather | solution.py:141
  45.3 0.1 pad_add_fusion.place
  45.4 1.2 %copy-done.3 = bf16[2048,256]{1,0:T(8,128)(2,1)S(1)} copy-done((bf16[2048,256]{1,0:T(8,128)(2,1)S(1)}, bf16[2048,256]{1,0:T(8,128)(2,1)}, u32[]{:S(2)}) %copy-start.3) | copy-done | bytes 1048600
  46.6 0.9 %copy-done.4 = bf16[512,256]{1,0:T(8,128)(2,1)S(1)} copy-done((bf16[512,256]{1,0:T(8,128)(2,1)S(1)}, bf16[512,256]{1,0:T(8,128)(2,1)}, u32[]{:S(2)}) %copy-start.4) | copy-done | bytes 262168
  47.5 2.4 %shard_map.73 = (f32[256,384]{1,0:T(8,128)S(1)}, bf16[256,384]{1,0:T(8,128)(2,1)S(1)}) custom-call(s32[2]{0:T(128)S(1)} %pad_add_fusion.place, bf16[8,256,256]{2,1,0:T(8,128)(2,1)S(1)} %all-to-all-done.x, bf16[2048,256]{1,0:T(8,128)(2,1)S(1)} %copy-done.2, bf16[2048,256]{1,0:T(8,128)(2,1)S(1)} %copy-done.3, bf16[2,256,256]{2,1,0:T(8,128)(2,1)S(1)} %bitcast.9, ...), custom_call_target="tpu_custom_call" | custom-call | tf_op jit(solution)/shard_map/pallas_call | solution.py:144
  49.9 2.2 %all-gather.1 = bf16[512,384]{1,0:T(8,128)(2,1)S(1)} all-gather(bf16[256,384]{1,0:T(8,128)(2,1)S(1)} %get-tuple-element.8), channel_id=3, replica_groups={{0,8},{16,24},{32,40},{48,56},{64,72},{80,88},{96,104},{112,120},{128,1..., dimensions={0}, use_global_device_ids=true | all-gather | bytes 589824 | tf_op jit(solution)/shard_map/all_gather | solution.py:153
  52.1 1.5 %shard_map.74 = bf16[256,384]{1,0:T(8,128)(2,1)S(1)} custom-call(s32[2]{0:T(128)S(1)} %pad_add_fusion.place, f32[256,384]{1,0:T(8,128)S(1)} %get-tuple-element.7.keep, bf16[2,256,384]{2,1,0:T(8,128)(2,1)S(1)} %bitcast.8), custom_call_target="tpu_custom_call" | custom-call | tf_op jit(solution)/shard_map/pallas_call | solution.py:154
  53.6 20.9 %all_to_all.15.got = bf16[32,8,384]{2,1,0:T(8,128)(2,1)S(1)} all-to-all(bf16[32,8,384]{2,1,0:T(8,128)(2,1)S(1)} %bitcast.10), channel_id=1, replica_groups={{0,16,32,48,64,80,96,112,128,144,160,176,192,208,224,240,256,272,288,30..., dimensions={0} | all-to-all | bytes 393216 | tf_op jit(solution)/shard_map/all_to_all | solution.py:157
  74.5 1.2 %shard_map.75 = f32[8,8,256]{2,1,0:T(8,128)} custom-call(bf16[32,8,384]{2,1,0:T(8,128)(2,1)S(1)} %all_to_all.15.got, bf16[256,2048]{1,0:T(8,128)(2,1)S(1)} %copy-done.1), custom_call_target="tpu_custom_call" | custom-call | tf_op jit(solution)/shard_map/pallas_call | solution.py:161
  75.7 7.3 %all-to-all-start.2 = ((f32[8,8,256]{2,1,0:T(8,128)}), f32[8,8,256]{2,1,0:T(8,128)S(1)}, u32[]{:S(2)}, u32[]{:S(2)}) async-start(f32[8,8,256]{2,1,0:T(8,128)} %shard_map.75), calls=%async_computation.2 | async-start | bytes 131072 | tf_op jit(solution)/shard_map/all_to_all | solution.py:164
  83.0 8.4 %all-to-all-done.2 = f32[8,8,256]{2,1,0:T(8,128)S(1)} async-done(((f32[8,8,256]{2,1,0:T(8,128)}), f32[8,8,256]{2,1,0:T(8,128)S(1)}, u32[]{:S(2)}, u32[]{:S(2)}) %all-to-all-start.2) | async-done | bytes 65568 | tf_op jit(solution)/shard_map/all_to_all | solution.py:164
  91.4 0.6 add_convert_fusion
  (13 shorter events, 0.0 us)
Async XLA Ops:
  0.0 10.1 %copy-start = (bf16[2048,256]{1,0:T(8,128)(2,1)S(1)}, bf16[2048,256]{1,0:T(8,128)(2,1)}, u32[]{:S(2)}) copy-start(bf16[2048,256]{1,0:T(8,128)(2,1)} %param.10) | copy-start | bytes 3145732
  2.0 43.3 %all-to-all-start = ((bf16[8,256,256]{2,1,0:T(8,128)(2,1)}), bf16[8,256,256]{2,1,0:T(8,128)(2,1)S(1)}, u32[]{:S(2)}, u32[]{:S(2)}) async-start(bf16[8,256,256]{2,1,0:T(8,128)(2,1)} %broadcast_in_dim.2), calls=%async_computation | async-start | bytes 2097152 | tf_op jit(solution)/shard_map/all_to_all | solution.py:131
  9.1 0.7 copy-start.6
  9.9 0.8 copy-start.5
  9.9 35.4 %copy-start.2 = (bf16[2048,256]{1,0:T(8,128)(2,1)S(1)}, bf16[2048,256]{1,0:T(8,128)(2,1)}, u32[]{:S(2)}) copy-start(bf16[2048,256]{1,0:T(8,128)(2,1)} %wk.1) | copy-start | bytes 3145732
  45.4 1.2 %copy-start.3 = (bf16[2048,256]{1,0:T(8,128)(2,1)S(1)}, bf16[2048,256]{1,0:T(8,128)(2,1)}, u32[]{:S(2)}) copy-start(bf16[2048,256]{1,0:T(8,128)(2,1)} %wv.1) | copy-start | bytes 3145732
  46.6 0.9 %copy-start.4 = (bf16[512,256]{1,0:T(8,128)(2,1)S(1)}, bf16[512,256]{1,0:T(8,128)(2,1)}, u32[]{:S(2)}) copy-start(bf16[512,256]{1,0:T(8,128)(2,1)} %all-gather) | copy-start | bytes 786436
  49.9 24.6 %copy-start.1 = (bf16[256,2048]{1,0:T(8,128)(2,1)S(1)}, bf16[256,2048]{1,0:T(8,128)(2,1)}, u32[]{:S(2)}) copy-start(bf16[256,2048]{1,0:T(8,128)(2,1)} %w_out.1) | copy-start | bytes 3145732
  75.7 15.7 %all-to-all-start.2 = ((f32[8,8,256]{2,1,0:T(8,128)}), f32[8,8,256]{2,1,0:T(8,128)S(1)}, u32[]{:S(2)}, u32[]{:S(2)}) async-start(f32[8,8,256]{2,1,0:T(8,128)} %shard_map.75), calls=%async_computation.2 | async-start | bytes 131072 | tf_op jit(solution)/shard_map/all_to_all | solution.py:164

commit v3 on v2

--- a/solution.py
+++ b/solution.py
@@ -8,6 +8,7 @@
 HD = 128
 META = 128
 CORES = 2
+LAST = 4
 BF = jnp.bfloat16
 F32 = jnp.float32
 LIMIT = 40 * 1024 * 1024
@@ -38,51 +39,39 @@
     return part[0] + (part[1] + part[2]), part[3] + (part[4] + part[5])
 
 
-def attend_kernel(place, x, wk, wv, q, lens, keep, send):
+def copies_kernel(context, out):
+    for d in range(out.shape[0]):
+        out[d] = context[...]
+
+
+def key_value_kernel(x, wk, wv, out):
+    width = wk.shape[1]
+    feats = jnp.concatenate([x[f] for f in range(x.shape[0])], axis=1)
+    out[:, :width] = jnp.dot(feats, wk[...], preferred_element_type=F32).astype(BF)
+    out[:, width:] = jnp.dot(feats, wv[...], preferred_element_type=F32).astype(BF)
+
+
+def attend_kernel(place, kv, q, lens, out):
     core, base = place[0], place[1]
-    heads = wk.shape[1] // HD
-    rows, width = q.shape[1], q.shape[2]
-    positions = x.shape[1]
-    feats = jnp.concatenate([x[f] for f in range(x.shape[0])], axis=1)
-    k = jnp.dot(feats, wk[...], preferred_element_type=F32).astype(BF)
-    v = jnp.dot(feats, wv[...], preferred_element_type=F32).astype(BF)
+    rows, width = q.shape
+    positions = kv.shape[0]
     ones = jnp.ones((positions, HD), BF)
     pos = base + lax.broadcasted_iota(jnp.int32, (rows, positions), 1)
-    for half, ref in ((1 - core, send), (core, keep)):
-        visible = pos < lens[half]
-        qh = q[half]
-        tops, totals = [], []
-        for h in range(heads):
-            cols = slice(h * HD, (h + 1) * HD)
-            s = lax.dot_general(
-                qh[:, cols], k[:, cols], (((1,), (1,)), ((), ())), preferred_element_type=F32
-            )
-            s = jnp.where(visible, s, -jnp.inf)
-            top = jnp.maximum(jnp.max(s, axis=1, keepdims=True), -1e30)
-            probs = jnp.exp(s - top).astype(BF)
-            both = jnp.dot(
-                probs, jnp.concatenate([v[:, cols], ones], axis=1), preferred_element_type=F32
-            )
-            ref[:, cols] = both[:, :HD].astype(ref.dtype)
-            tops.append(top)
-            totals.append(both[:, HD : HD + 1])
-        ref[:, width:] = pack_meta(tops, totals).astype(ref.dtype)
-
-
-def pair_kernel(place, keep, got, out):
-    other = 1 - place[0]
-    width = keep.shape[1] - META
-    theirs = got[other]
+    visible = pos < lens[core]
     tops, totals = [], []
     for h in range(width // HD):
         cols = slice(h * HD, (h + 1) * HD)
-        top_a, total_a = read_meta(keep[:, width:], h)
-        top_b, total_b = read_meta(theirs[:, width:], h)
-        top = jnp.maximum(top_a, top_b)
-        scale_a, scale_b = jnp.exp(top_a - top), jnp.exp(top_b - top)
-        out[:, cols] = (scale_a * keep[:, cols] + scale_b * theirs[:, cols].astype(F32)).astype(BF)
+        s = lax.dot_general(
+            q[:, cols], kv[:, cols], (((1,), (1,)), ((), ())), preferred_element_type=F32
+        )
+        s = jnp.where(visible, s, -jnp.inf)
+        top = jnp.maximum(jnp.max(s, axis=1, keepdims=True), -1e30)
+        probs = jnp.exp(s - top).astype(BF)
+        v = kv[:, width + h * HD : width + (h + 1) * HD]
+        both = jnp.dot(probs, jnp.concatenate([v, ones], axis=1), preferred_element_type=F32)
+        out[:, cols] = both[:, :HD].astype(BF)
         tops.append(top)
-        totals.append(scale_a * total_a + scale_b * total_b)
+        totals.append(both[:, HD : HD + 1])
     out[:, width:] = pack_meta(tops, totals)
 
 
@@ -124,35 +113,34 @@
     half = chips * lat_dev
     qscale = 1.0 / HD**0.5
     me = lax.axis_index("ctx")
-    place = jnp.stack([me % CORES, me * ctx_dev]).astype(jnp.int32)
+    place = jnp.stack([me % CORES, (me // CORES) * (CORES * ctx_dev)]).astype(jnp.int32)
     same_core = [[c + CORES * g for g in range(chips)] for c in range(CORES)]
     core_pairs = [[CORES * g + c for c in range(CORES)] for g in range(chips)]
 
-    x = lax.all_to_all(
-        jnp.broadcast_to(context[None], (heads_axis,) + context.shape), "head", 0, 0
-    )
+    copies = call(
+        copies_kernel, jax.ShapeDtypeStruct((heads_axis,) + context.shape, BF), 1, False
+    )(context)
+    x = lax.all_to_all(copies, "head", 0, 0)
 
     q = (jnp.dot(latents, w_query, preferred_element_type=F32) * qscale).astype(BF)
+    last = min(LAST, chips)
     bit = CORES
-    while bit < groups:
+    while bit < groups // last:
         pairs = [[i, i | bit] for i in range(groups) if not i & bit]
         q = lax.all_gather(q, "ctx", axis=0, tiled=True, axis_index_groups=pairs)
         bit *= 2
-    q = lax.all_gather(q, "ctx", axis=0, axis_index_groups=core_pairs)
+    far = [[i + bit * j for j in range(last)] for i in range(bit)]
+    q = lax.all_to_all(
+        jnp.broadcast_to(q[None], (last,) + q.shape), "ctx", 0, 0, axis_index_groups=far
+    ).reshape(half, width)
     lens = lengths.reshape(chips, CORES, lat_dev).transpose(1, 0, 2).reshape(CORES, half, 1)
 
-    keep, send = call(
-        attend_kernel,
-        [
-            jax.ShapeDtypeStruct((half, width + META), F32),
-            jax.ShapeDtypeStruct((half, width + META), BF),
-        ],
-        6,
-        True,
-    )(place, x, w_key, w_value, q, lens)
-    got = lax.all_gather(send, "ctx", axis=0, axis_index_groups=core_pairs)
-    paired = call(pair_kernel, jax.ShapeDtypeStruct((half, width + META), BF), 3, True)(
-        place, keep, got
+    kv = call(key_value_kernel, jax.ShapeDtypeStruct((ctx_dev, 2 * width), BF), 3, False)(
+        x, w_key, w_value
+    )
+    kv = lax.all_gather(kv, "ctx", axis=0, tiled=True, axis_index_groups=core_pairs)
+    paired = call(attend_kernel, jax.ShapeDtypeStruct((half, width + META), BF), 4, True)(
+        place, kv, q, lens
     )
     got = lax.all_to_all(
         paired.reshape(chips, lat_dev, width + META), "ctx", 0, 0, axis_index_groups=same_core

time: 92.8 us -> 90.1 us (0.971)
  blocking collectives: 57.4 us -> 32.5 us
  waiting for transfers between devices: 8.38 us -> 26.6 us
  starting transfers between devices: 14.4 us -> 20.9 us
  local copies, waits for them, and re-layouts: 5.7 us -> 3.12 us
    all_to_all x1 -> x2, waiting for transfers between devices: 0.01 us -> 18.4 us  [the longest x1 13.2 us: on_device(): x = lax.all_to_all(copies, 'head', 0, 0)]
    all_gather x5 -> x3, blocking collectives: 32.2 us -> 14.9 us  [on_device(): q = lax.all_gather(q, 'ctx', axis=0, tiled=True, axis_index_groups=pairs)]
    all_to_all x1 -> x2, starting transfers between devices: 7.1 us -> 17.5 us  [the longest x1 10.3 us: on_device(): lax.all_to_all(jnp.broadcast_to(q[None], (last,) + q.shape), 'ctx', 0, 0,...]
    all_to_all x1, blocking collectives: 20.9 us -> 15.3 us  [on_device(): lax.all_to_all(paired.reshape(chips, lat_dev, width + META), 'ctx', 0, 0,...]
    all_to_all x1, starting transfers between devices: 7.33 us -> 3.35 us  [on_device(): summed = jnp.sum(lax.all_to_all(shares, 'head', 0, 0), axis=0)]
    all_gather x2 -> x1, blocking collectives: 4.33 us -> 2.31 us  [on_device(): lax.all_gather(kv, 'ctx', axis=0, tiled=True, axis_index_groups=core_pairs)]
    broadcast_in_dim x1, local copies, waits for them, and re-layouts: 2.02 us -> 0.65 us  [on_device(): jnp.broadcast_to(q[None], (last,) + q.shape)]
    unnamed x14, local copies, waits for them, and re-layouts: 3.45 us -> 2.24 us
  transfers between devices with their start and end apart: 2 -> 3, of which waited for: 1 -> 3; matrix products, arithmetic and copies ran while one was open for 1% -> 1% of each run, Pallas kernels for 0% -> 1%
where the time goes in v3:
time: 90.1 us; the launch traced here: 89.2 us
  blocking collectives  32.5 us (36%)
  waiting for transfers between devices  26.6 us (30%)
  starting transfers between devices  20.9 us (23%)
  Pallas kernels  4.27 us (5%)
  local copies, waits for them, and re-layouts  3.12 us (3%)
  other arithmetic  1.37 us (2%)
    all_to_all x1, blocking collectives, on_device(): lax.all_to_all(paired.reshape(chips, lat_dev, width + META), 'ctx', 0, 0,...  15.3 us
    all_gather x3, blocking collectives, on_device(): q = lax.all_gather(q, 'ctx', axis=0, tiled=True, axis_index_groups=pairs)  14.9 us
    all_to_all x1, waiting for transfers between devices, on_device(): x = lax.all_to_all(copies, 'head', 0, 0)  13.2 us
    all_to_all x1, starting transfers between devices, on_device(): lax.all_to_all(jnp.broadcast_to(q[None], (last,) + q.shape), 'ctx', 0, 0,...  10.3 us
    all_to_all x1, waiting for transfers between devices, on_device(): summed = jnp.sum(lax.all_to_all(shares, 'head', 0, 0), axis=0)  8.29 us
    all_to_all x1, starting transfers between devices, on_device(): x = lax.all_to_all(copies, 'head', 0, 0)  7.23 us
    all_to_all x1, waiting for transfers between devices, on_device(): lax.all_to_all(jnp.broadcast_to(q[None], (last,) + q.shape), 'ctx', 0, 0,...  5.12 us
    all_to_all x1, starting transfers between devices, on_device(): summed = jnp.sum(lax.all_to_all(shares, 'head', 0, 0), axis=0)  3.35 us
  transfers between devices with their start and end apart: 3, of which 3 were waited for; matrix products, arithmetic and copies ran while one was open for 1% of the time, Pallas kernels for 1%

profile of v3, /device:TPU:6, one launch (start us, length us, event | category | flops | bytes accessed | tf_op | source)
XLA Modules:
  0.0 89.2 jit_solution(2438651922050750017)
XLA Ops:
  0.0 1.0 %copy-done.4 = bf16[256,256]{1,0:T(8,128)(2,1)S(1)} copy-done((bf16[256,256]{1,0:T(8,128)(2,1)S(1)}, bf16[256,256]{1,0:T(8,128)(2,1)}, u32[]{:S(2)}) %copy-start.4) | copy-done | bytes 131096
  1.0 1.0 %shard_map.73 = bf16[8,256,256]{2,1,0:T(8,128)(2,1)} custom-call(bf16[256,256]{1,0:T(8,128)(2,1)S(1)} %copy-done.4), custom_call_target="tpu_custom_call" | custom-call | tf_op jit(solution)/shard_map/pallas_call | solution.py:120
  2.0 7.2 %all-to-all-start = ((bf16[8,256,256]{2,1,0:T(8,128)(2,1)}), bf16[8,256,256]{2,1,0:T(8,128)(2,1)S(1)}, u32[]{:S(2)}, u32[]{:S(2)}) async-start(bf16[8,256,256]{2,1,0:T(8,128)(2,1)} %shard_map.73), calls=%async_computation | async-start | bytes 2097152 | tf_op jit(solution)/shard_map/all_to_all | solution.py:123
  9.3 0.1 reshape.14
  9.4 0.1 reshape.17.lens
  9.6 0.2 fusion
  9.8 4.3 %all_gather.13 = bf16[16,256]{1,0:T(8,128)(2,1)S(1)} all-gather(bf16[8,256]{1,0:T(8,128)(2,1)S(1)} %fusion), channel_id=1, replica_groups={{0,16},{8,24},{32,48},{40,56},{64,80},{72,88},{96,112},{104,120},{128,1..., dimensions={0}, use_global_device_ids=true | all-gather | bytes 12288 | tf_op jit(solution)/shard_map/all_gather | solution.py:130
  14.2 5.9 %all_gather.14 = bf16[32,256]{1,0:T(8,128)(2,1)S(1)} all-gather(bf16[16,256]{1,0:T(8,128)(2,1)S(1)} %all_gather.13), channel_id=1, replica_groups={{0,32},{8,40},{16,48},{24,56},{64,96},{72,104},{80,112},{88,120},{128,1..., dimensions={0}, use_global_device_ids=true | all-gather | bytes 24576 | tf_op jit(solution)/shard_map/all_gather | solution.py:130
  20.0 4.7 %all_gather.15 = bf16[64,256]{1,0:T(8,128)(2,1)S(1)} all-gather(bf16[32,256]{1,0:T(8,128)(2,1)S(1)} %all_gather.14), channel_id=1, replica_groups={{0,64},{8,72},{16,80},{24,88},{32,96},{40,104},{48,112},{56,120},{128,1..., dimensions={0}, use_global_device_ids=true | all-gather | bytes 49152 | tf_op jit(solution)/shard_map/all_gather | solution.py:130
  24.8 13.2 %all-to-all-done.x = bf16[8,256,256]{2,1,0:T(8,128)(2,1)S(1)} async-done(((bf16[8,256,256]{2,1,0:T(8,128)(2,1)}), bf16[8,256,256]{2,1,0:T(8,128)(2,1)S(1)}, u32[]{:S(2)}, u32[]{:S(2)}) %all-to-all-start) | async-done | bytes 1048608 | tf_op jit(solution)/shard_map/all_to_all | solution.py:123
  38.0 0.7 broadcast_in_dim.2
  38.7 10.3 %all-to-all-start.1 = ((bf16[4,64,256]{2,1,0:T(8,128)(2,1)}), bf16[4,64,256]{2,1,0:T(8,128)(2,1)S(1)}, u32[]{:S(2)}, u32[]{:S(2)}) async-start(bf16[4,64,256]{2,1,0:T(8,128)(2,1)} %broadcast_in_dim.2), calls=%async_computation.1 | async-start | bytes 262144 | tf_op jit(solution)/shard_map/all_to_all | solution.py:133
  49.0 0.1 pad_add_fusion.place
  49.0 1.2 %copy-done.3 = bf16[2048,256]{1,0:T(8,128)(2,1)S(1)} copy-done((bf16[2048,256]{1,0:T(8,128)(2,1)S(1)}, bf16[2048,256]{1,0:T(8,128)(2,1)}, u32[]{:S(2)}) %copy-start.3) | copy-done | bytes 1048600
  50.3 0.7 shard_map.74
  51.0 0.0 copy-start.1
  51.0 2.3 %all_gather.12.kv = bf16[512,512]{1,0:T(8,128)(2,1)S(1)} all-gather(bf16[256,512]{1,0:T(8,128)(2,1)S(1)} %shard_map.74), channel_id=1, replica_groups={{0,8},{16,24},{32,40},{48,56},{64,72},{80,88},{96,104},{112,120},{128,1..., dimensions={0}, use_global_device_ids=true | all-gather | bytes 786432 | tf_op jit(solution)/shard_map/all_gather | solution.py:141
  53.3 5.1 %all-to-all-done.1 = bf16[4,64,256]{2,1,0:T(8,128)(2,1)S(1)} async-done(((bf16[4,64,256]{2,1,0:T(8,128)(2,1)}), bf16[4,64,256]{2,1,0:T(8,128)(2,1)S(1)}, u32[]{:S(2)}, u32[]{:S(2)}) %all-to-all-start.1) | async-done | bytes 131104 | tf_op jit(solution)/shard_map/all_to_all | solution.py:133
  58.4 1.3 %shard_map.75 = bf16[256,384]{1,0:T(8,128)(2,1)S(1)} custom-call(s32[2]{0:T(128)S(1)} %pad_add_fusion.place, bf16[512,512]{1,0:T(8,128)(2,1)S(1)} %all_gather.12.kv, bf16[256,256]{1,0:T(8,128)(2,1)S(1)} %bitcast.8, s32[2,256,1]{2,1,0:T(8,128)S(1)} %reshape.17.lens), custom_call_target="tpu_custom_call" | custom-call | tf_op jit(solution)/shard_map/pallas_call | solution.py:142
  59.7 15.3 %all_to_all.20.got = bf16[32,8,384]{2,1,0:T(8,128)(2,1)S(1)} all-to-all(bf16[32,8,384]{2,1,0:T(8,128)(2,1)S(1)} %bitcast.7), channel_id=1, replica_groups={{0,16,32,48,64,80,96,112,128,144,160,176,192,208,224,240,256,272,288,30..., dimensions={0} | all-to-all | bytes 393216 | tf_op jit(solution)/shard_map/all_to_all | solution.py:145
  75.0 1.2 %shard_map.76 = f32[8,8,256]{2,1,0:T(8,128)} custom-call(bf16[32,8,384]{2,1,0:T(8,128)(2,1)S(1)} %all_to_all.20.got, bf16[256,2048]{1,0:T(8,128)(2,1)S(1)} %copy-done.1), custom_call_target="tpu_custom_call" | custom-call | tf_op jit(solution)/shard_map/pallas_call | solution.py:149
  76.2 3.3 %all-to-all-start.3 = ((f32[8,8,256]{2,1,0:T(8,128)}), f32[8,8,256]{2,1,0:T(8,128)S(1)}, u32[]{:S(2)}, u32[]{:S(2)}) async-start(f32[8,8,256]{2,1,0:T(8,128)} %shard_map.76), calls=%async_computation.3 | async-start | bytes 131072 | tf_op jit(solution)/shard_map/all_to_all | solution.py:152
  79.6 8.3 %all-to-all-done.3 = f32[8,8,256]{2,1,0:T(8,128)S(1)} async-done(((f32[8,8,256]{2,1,0:T(8,128)}), f32[8,8,256]{2,1,0:T(8,128)S(1)}, u32[]{:S(2)}, u32[]{:S(2)}) %all-to-all-start.3) | async-done | bytes 65568 | tf_op jit(solution)/shard_map/all_to_all | solution.py:152
  87.9 1.3 %add_convert_fusion = bf16[8,256]{1,0:T(8,128)(2,1)} fusion(f32[8,256]{1,0:T(8,128)S(1)} %reduce_sum.9, bf16[8,2048]{1,0:T(8,128)(2,1)} %param.7, s32[]{:T(128)S(6)} %select_n.14), kind=kLoop, calls=%fused_computation.2 | loop fusion | flops 6144 | bytes 16388 | tf_op jit(solution)/shard_map/convert_element_type | solution.py:155
  (13 shorter events, 0.0 us)
Async XLA Ops:
  0.0 9.6 %copy-start = (bf16[2048,256]{1,0:T(8,128)(2,1)S(1)}, bf16[2048,256]{1,0:T(8,128)(2,1)}, u32[]{:S(2)}) copy-start(bf16[2048,256]{1,0:T(8,128)(2,1)} %param.10) | copy-start | bytes 3145732
  0.0 1.0 %copy-start.4 = (bf16[256,256]{1,0:T(8,128)(2,1)S(1)}, bf16[256,256]{1,0:T(8,128)(2,1)}, u32[]{:S(2)}) copy-start(bf16[256,256]{1,0:T(8,128)(2,1)} %context.1) | copy-start | bytes 393220
  2.0 7.3 %copy-start.6 = (s32[512]{0:T(512)S(1)}, s32[512]{0:T(512)}, u32[]{:S(2)}) copy-start(s32[512]{0:T(512)} %param.9) | copy-start | bytes 6148
  2.0 7.6 %copy-start.5 = (bf16[8,2048]{1,0:T(8,128)(2,1)S(1)}, bf16[8,2048]{1,0:T(8,128)(2,1)}, u32[]{:S(2)}) copy-start(bf16[8,2048]{1,0:T(8,128)(2,1)} %param.7) | copy-start | bytes 98308
  2.0 36.0 %all-to-all-start = ((bf16[8,256,256]{2,1,0:T(8,128)(2,1)}), bf16[8,256,256]{2,1,0:T(8,128)(2,1)S(1)}, u32[]{:S(2)}, u32[]{:S(2)}) async-start(bf16[8,256,256]{2,1,0:T(8,128)(2,1)} %shard_map.73), calls=%async_computation | async-start | bytes 2097152 | tf_op jit(solution)/shard_map/all_to_all | solution.py:123
  9.3 39.8 %copy-start.2 = (bf16[2048,256]{1,0:T(8,128)(2,1)S(1)}, bf16[2048,256]{1,0:T(8,128)(2,1)}, u32[]{:S(2)}) copy-start(bf16[2048,256]{1,0:T(8,128)(2,1)} %wk.1) | copy-start | bytes 3145732
  38.7 19.8 %all-to-all-start.1 = ((bf16[4,64,256]{2,1,0:T(8,128)(2,1)}), bf16[4,64,256]{2,1,0:T(8,128)(2,1)S(1)}, u32[]{:S(2)}, u32[]{:S(2)}) async-start(bf16[4,64,256]{2,1,0:T(8,128)(2,1)} %broadcast_in_dim.2), calls=%async_computation.1 | async-start | bytes 262144 | tf_op jit(solution)/shard_map/all_to_all | solution.py:133
  49.0 1.2 %copy-start.3 = (bf16[2048,256]{1,0:T(8,128)(2,1)S(1)}, bf16[2048,256]{1,0:T(8,128)(2,1)}, u32[]{:S(2)}) copy-start(bf16[2048,256]{1,0:T(8,128)(2,1)} %wv.1) | copy-start | bytes 3145732
  51.0 24.0 %copy-start.1 = (bf16[256,2048]{1,0:T(8,128)(2,1)S(1)}, bf16[256,2048]{1,0:T(8,128)(2,1)}, u32[]{:S(2)}) copy-start(bf16[256,2048]{1,0:T(8,128)(2,1)} %w_out.1) | copy-start | bytes 3145732
  76.2 11.7 %all-to-all-start.3 = ((f32[8,8,256]{2,1,0:T(8,128)}), f32[8,8,256]{2,1,0:T(8,128)S(1)}, u32[]{:S(2)}, u32[]{:S(2)}) async-start(f32[8,8,256]{2,1,0:T(8,128)} %shard_map.76), calls=%async_computation.3 | async-start | bytes 131072 | tf_op jit(solution)/shard_map/all_to_all | solution.py:152

commit v4 on v3

--- a/solution.py
+++ b/solution.py
@@ -8,7 +8,7 @@
 HD = 128
 META = 128
 CORES = 2
-LAST = 4
+FAR = (4, 3, 1, 2, 0)
 BF = jnp.bfloat16
 F32 = jnp.float32
 LIMIT = 40 * 1024 * 1024
@@ -39,15 +39,21 @@
     return part[0] + (part[1] + part[2]), part[3] + (part[4] + part[5])
 
 
-def copies_kernel(context, out):
-    for d in range(out.shape[0]):
-        out[d] = context[...]
+def copies_kernel(context, out, sems):
+    copies = [pltpu.make_async_copy(context, out.at[d], sems.at[d]) for d in range(out.shape[0])]
+    for copy in copies:
+        copy.start()
+    for copy in copies:
+        copy.wait()
 
 
-def key_value_kernel(x, wk, wv, out):
+def key_value_kernel(x, wk, wv_hbm, out, wv, sem):
     width = wk.shape[1]
+    fetch = pltpu.make_async_copy(wv_hbm, wv, sem)
+    fetch.start()
     feats = jnp.concatenate([x[f] for f in range(x.shape[0])], axis=1)
     out[:, :width] = jnp.dot(feats, wk[...], preferred_element_type=F32).astype(BF)
+    fetch.wait()
     out[:, width:] = jnp.dot(feats, wv[...], preferred_element_type=F32).astype(BF)
 
 
@@ -89,16 +95,25 @@
         out[d] = projected[:, d * cols : (d + 1) * cols]
 
 
-def call(kernel, shapes, n_in, smem_first):
-    vmem = pl.BlockSpec(memory_space=pltpu.VMEM)
-    specs = [vmem] * n_in
-    if smem_first:
-        specs[0] = pl.BlockSpec(memory_space=pltpu.SMEM)
+def finish_kernel(place, shares, latents, out):
+    cols = out.shape[1]
+    first = pl.multiple_of(place[2] * cols, cols)
+    summed = jnp.sum(shares[...], axis=0)
+    out[...] = (latents[:, pl.ds(first, cols)].astype(F32) + summed).astype(BF)
+
+
+VMEM = pl.BlockSpec(memory_space=pltpu.VMEM)
+SMEM = pl.BlockSpec(memory_space=pltpu.SMEM)
+HBM = pl.BlockSpec(memory_space=pltpu.HBM)
+
+
+def call(kernel, shape, dtype, in_specs, out_spec=VMEM, scratch=()):
     return pl.pallas_call(
         kernel,
-        out_shape=shapes,
-        in_specs=specs,
-        out_specs=jax.tree.map(lambda _: vmem, shapes),
+        out_shape=jax.ShapeDtypeStruct(shape, dtype),
+        in_specs=in_specs,
+        out_specs=out_spec,
+        scratch_shapes=scratch,
         compiler_params=pltpu.CompilerParams(vmem_limit_bytes=LIMIT),
     )
 
@@ -113,46 +128,55 @@
     half = chips * lat_dev
     qscale = 1.0 / HD**0.5
     me = lax.axis_index("ctx")
-    place = jnp.stack([me % CORES, (me // CORES) * (CORES * ctx_dev)]).astype(jnp.int32)
-    same_core = [[c + CORES * g for g in range(chips)] for c in range(CORES)]
-    core_pairs = [[CORES * g + c for c in range(CORES)] for g in range(chips)]
+    my_head = lax.axis_index("head")
+    place = jnp.stack([me % CORES, (me // CORES) * (CORES * ctx_dev), my_head]).astype(jnp.int32)
 
     copies = call(
-        copies_kernel, jax.ShapeDtypeStruct((heads_axis,) + context.shape, BF), 1, False
-    )(context)
+        copies_kernel,
+        (heads_axis,) + context.shape,
+        BF,
+        [HBM],
+        HBM,
+        [pltpu.SemaphoreType.DMA((heads_axis,))],
+    )(pltpu.with_memory_space_constraint(context, pltpu.HBM))
     x = lax.all_to_all(copies, "head", 0, 0)
 
     q = (jnp.dot(latents, w_query, preferred_element_type=F32) * qscale).astype(BF)
-    last = min(LAST, chips)
-    bit = CORES
-    while bit < groups // last:
-        pairs = [[i, i | bit] for i in range(groups) if not i & bit]
+    bits = chips.bit_length() - 1
+    order = sorted(range(bits), key=FAR.index)
+    places = [0]
+    for b in order:
+        step = CORES << b
+        pairs = [[i, i | step] for i in range(groups) if not i & step]
         q = lax.all_gather(q, "ctx", axis=0, tiled=True, axis_index_groups=pairs)
-        bit *= 2
-    far = [[i + bit * j for j in range(last)] for i in range(bit)]
-    q = lax.all_to_all(
-        jnp.broadcast_to(q[None], (last,) + q.shape), "ctx", 0, 0, axis_index_groups=far
-    ).reshape(half, width)
-    lens = lengths.reshape(chips, CORES, lat_dev).transpose(1, 0, 2).reshape(CORES, half, 1)
+        places = places + [p | step for p in places]
+    same_core = [[c + p for p in places] for c in range(CORES)]
+    core_pairs = [[CORES * g + c for c in range(CORES)] for g in range(chips)]
+    lens = lengths.reshape((2,) * bits + (CORES, lat_dev))
+    lens = lens.transpose([bits] + [bits - 1 - b for b in reversed(order)] + [bits + 1])
+    lens = lens.reshape(CORES, half, 1)
 
-    kv = call(key_value_kernel, jax.ShapeDtypeStruct((ctx_dev, 2 * width), BF), 3, False)(
-        x, w_key, w_value
-    )
+    kv = call(
+        key_value_kernel,
+        (ctx_dev, 2 * width),
+        BF,
+        [VMEM, VMEM, HBM],
+        VMEM,
+        [pltpu.VMEM(w_value.shape, BF), pltpu.SemaphoreType.DMA],
+    )(x, w_key, pltpu.with_memory_space_constraint(w_value, pltpu.HBM))
     kv = lax.all_gather(kv, "ctx", axis=0, tiled=True, axis_index_groups=core_pairs)
-    paired = call(attend_kernel, jax.ShapeDtypeStruct((half, width + META), BF), 4, True)(
+    part = call(attend_kernel, (half, width + META), BF, [SMEM, VMEM, VMEM, VMEM])(
         place, kv, q, lens
     )
     got = lax.all_to_all(
-        paired.reshape(chips, lat_dev, width + META), "ctx", 0, 0, axis_index_groups=same_core
+        part.reshape(chips, lat_dev, width + META), "ctx", 0, 0, axis_index_groups=same_core
     )
     cols_dev = w_out.shape[1] // heads_axis
-    shares = call(
-        project_kernel, jax.ShapeDtypeStruct((heads_axis, lat_dev, cols_dev), F32), 2, False
-    )(got, w_out)
-    summed = jnp.sum(lax.all_to_all(shares, "head", 0, 0), axis=0)
-    first_col = lax.axis_index("head") * cols_dev
-    residual = lax.dynamic_slice_in_dim(latents, first_col, cols_dev, 1).astype(F32)
-    return (residual + summed).astype(BF)
+    shares = call(project_kernel, (heads_axis, lat_dev, cols_dev), F32, [VMEM, VMEM])(got, w_out)
+    shares = lax.all_to_all(shares, "head", 0, 0)
+    return call(finish_kernel, (lat_dev, cols_dev), BF, [SMEM, VMEM, VMEM])(
+        place, shares, latents
+    )
 
 
 def solution(mesh):

time: 90.1 us -> 117 us (1.30)
  blocking collectives: 32.5 us -> 71 us
  Pallas kernels: 4.27 us -> 37.9 us
  waiting for transfers between devices: 26.6 us -> 0.01 us
  starting transfers between devices: 20.9 us -> 7.11 us
  local copies, waits for them, and re-layouts: 3.12 us -> 0.31 us
  other arithmetic: 1.37 us -> 0.08 us
    pallas_call x4 -> x5, Pallas kernels: 4.27 us -> 37.9 us  [the longest x1 32.9 us: on_device(): call(copies_kernel, (heads_axis,) + context.shape, BF, [HBM], HBM, [pltpu...]
    all_to_all x1 -> x2, blocking collectives: 15.3 us -> 36.7 us  [the longest x1 21.3 us: on_device(): lax.all_to_all(part.reshape(chips, lat_dev, width + META), 'ctx', 0, 0, a...]
    all_gather x3 -> x5, blocking collectives: 14.9 us -> 32 us  [on_device(): q = lax.all_gather(q, 'ctx', axis=0, tiled=True, axis_index_groups=pairs)]
    all_to_all x2 -> x0, starting transfers between devices: 13.6 us -> none  [the longest x1 10.3 us: on_device(): lax.all_to_all(jnp.broadcast_to(q[None], (last,) + q.shape), 'ctx', 0, 0,...]
    all_to_all x2 -> x0, waiting for transfers between devices: 13.4 us -> none  [the longest x1 8.29 us: on_device(): summed = jnp.sum(lax.all_to_all(shares, 'head', 0, 0), axis=0)]
    all_to_all x1, waiting for transfers between devices: 13.2 us -> 0.01 us  [on_device(): x = lax.all_to_all(copies, 'head', 0, 0)]
    unnamed x14 -> x12, local copies, waits for them, and re-layouts: 2.24 us -> 0.03 us
    convert_element_type x1 -> x0, other arithmetic: 1.29 us -> none  [on_device(): return (residual + summed).astype(BF)]
  transfers between devices with their start and end apart: 3 -> 1, of which waited for: 3 -> 0; matrix products, arithmetic and copies ran while one was open for 1% -> 1% of each run, Pallas kernels for 1% -> 0%
where the time goes in v4:
time: 117 us
  blocking collectives  71 us (61%)
  Pallas kernels  37.9 us (32%)
  starting transfers between devices  7.11 us (6%)
    pallas_call x1, Pallas kernels, on_device(): call(copies_kernel, (heads_axis,) + context.shape, BF, [HBM], HBM, [pltpu...  32.9 us
    all_gather x5, blocking collectives, on_device(): q = lax.all_gather(q, 'ctx', axis=0, tiled=True, axis_index_groups=pairs)  32 us
    all_to_all x1, blocking collectives, on_device(): lax.all_to_all(part.reshape(chips, lat_dev, width + META), 'ctx', 0, 0, a...  21.3 us
    all_to_all x1, blocking collectives, on_device(): shares = lax.all_to_all(shares, 'head', 0, 0)  15.5 us
    all_to_all x1, starting transfers between devices, on_device(): x = lax.all_to_all(copies, 'head', 0, 0)  7.11 us
  transfers between devices with their start and end apart: 1, of which 0 were waited for; matrix products, arithmetic and copies ran while one was open for 1% of the time, Pallas kernels for 0%

profile of v4, /device:TPU:6, one launch (start us, length us, event | category | flops | bytes accessed | tf_op | source)
XLA Modules:
  0.0 116.8 jit_solution(11575845291385776272)
XLA Ops:
  0.0 0.0 copy-start
  0.0 32.9 %shard_map.73 = bf16[8,256,256]{2,1,0:T(8,128)(2,1)} custom-call(bf16[256,256]{1,0:T(8,128)(2,1)} %context.1), custom_call_target="tpu_custom_call" | custom-call | tf_op jit(solution)/shard_map/pallas_call | solution.py:134
  32.9 0.0 copy-start.5
  33.0 0.0 copy-start.3
  33.0 7.1 %all-to-all-start = ((bf16[8,256,256]{2,1,0:T(8,128)(2,1)}), bf16[8,256,256]{2,1,0:T(8,128)(2,1)S(1)}, u32[]{:S(2)}, u32[]{:S(2)}) async-start(bf16[8,256,256]{2,1,0:T(8,128)(2,1)} %shard_map.73), calls=%async_computation | async-start | bytes 2097152 | tf_op jit(solution)/shard_map/all_to_all | solution.py:142
  40.1 0.0 copy-done.5
  40.1 0.1 reshape.9
  40.3 0.1 reshape.12.lens
  40.5 0.2 fusion
  40.7 11.3 %all_gather.19 = bf16[16,256]{1,0:T(8,128)(2,1)S(1)} all-gather(bf16[8,256]{1,0:T(8,128)(2,1)S(1)} %fusion), channel_id=1, replica_groups={{0,256},{8,264},{16,272},{24,280},{32,288},{40,296},{48,304},{56,312},{..., dimensions={0}, use_global_device_ids=true | all-gather | bytes 12288 | tf_op jit(solution)/shard_map/all_gather | solution.py:151
  52.0 5.3 %all_gather.20 = bf16[32,256]{1,0:T(8,128)(2,1)S(1)} all-gather(bf16[16,256]{1,0:T(8,128)(2,1)S(1)} %all_gather.19), channel_id=1, replica_groups={{0,128},{8,136},{16,144},{24,152},{32,160},{40,168},{48,176},{56,184},{..., dimensions={0}, use_global_device_ids=true | all-gather | bytes 24576 | tf_op jit(solution)/shard_map/all_gather | solution.py:151
  57.2 5.9 %all_gather.21 = bf16[64,256]{1,0:T(8,128)(2,1)S(1)} all-gather(bf16[32,256]{1,0:T(8,128)(2,1)S(1)} %all_gather.20), channel_id=1, replica_groups={{0,32},{8,40},{16,48},{24,56},{64,96},{72,104},{80,112},{88,120},{128,1..., dimensions={0}, use_global_device_ids=true | all-gather | bytes 49152 | tf_op jit(solution)/shard_map/all_gather | solution.py:151
  63.2 4.6 %all_gather.22 = bf16[128,256]{1,0:T(8,128)(2,1)S(1)} all-gather(bf16[64,256]{1,0:T(8,128)(2,1)S(1)} %all_gather.21), channel_id=1, replica_groups={{0,64},{8,72},{16,80},{24,88},{32,96},{40,104},{48,112},{56,120},{128,1..., dimensions={0}, use_global_device_ids=true | all-gather | bytes 98304 | tf_op jit(solution)/shard_map/all_gather | solution.py:151
  67.7 4.9 %all_gather.23.q = bf16[256,256]{1,0:T(8,128)(2,1)S(1)} all-gather(bf16[128,256]{1,0:T(8,128)(2,1)S(1)} %all_gather.22), channel_id=1, replica_groups={{0,16},{8,24},{32,48},{40,56},{64,80},{72,88},{96,112},{104,120},{128,1..., dimensions={0}, use_global_device_ids=true | all-gather | bytes 196608 | tf_op jit(solution)/shard_map/all_gather | solution.py:151
  72.7 0.1 pad_add_fusion.place
  72.7 0.0 all-to-all-done.x
  72.7 1.9 %shard_map.74 = bf16[256,512]{1,0:T(8,128)(2,1)S(1)} custom-call(bf16[8,256,256]{2,1,0:T(8,128)(2,1)S(1)} %all-to-all-done.x, bf16[2048,256]{1,0:T(8,128)(2,1)S(1)} %copy-done.2, bf16[2048,256]{1,0:T(8,128)(2,1)} %wv_hbm.1), custom_call_target="tpu_custom_call" | custom-call | tf_op jit(solution)/shard_map/pallas_call | solution.py:159
  74.7 0.0 copy-start.1
  74.7 2.3 %all_gather.18.kv = bf16[512,512]{1,0:T(8,128)(2,1)S(1)} all-gather(bf16[256,512]{1,0:T(8,128)(2,1)S(1)} %shard_map.74), channel_id=1, replica_groups={{0,8},{16,24},{32,40},{48,56},{64,72},{80,88},{96,104},{112,120},{128,1..., dimensions={0}, use_global_device_ids=true | all-gather | bytes 786432 | tf_op jit(solution)/shard_map/all_gather | solution.py:167
  77.0 1.3 %shard_map.75 = bf16[256,384]{1,0:T(8,128)(2,1)S(1)} custom-call(s32[3]{0:T(128)S(1)} %pad_add_fusion.place, bf16[512,512]{1,0:T(8,128)(2,1)S(1)} %all_gather.18.kv, bf16[256,256]{1,0:T(8,128)(2,1)S(1)} %all_gather.23.q, s32[2,256,1]{2,1,0:T(8,128)S(1)} %reshape.12.lens), custom_call_target="tpu_custom_call" | custom-call | tf_op jit(solution)/shard_map/pallas_call | solution.py:168
  78.3 21.3 %all_to_all.15.got = bf16[32,8,384]{2,1,0:T(8,128)(2,1)S(1)} all-to-all(bf16[32,8,384]{2,1,0:T(8,128)(2,1)S(1)} %bitcast.7), channel_id=1, replica_groups={{0,256,128,384,32,288,160,416,64,320,192,448,96,352,224,480,16,272,144,..., dimensions={0} | all-to-all | bytes 393216 | tf_op jit(solution)/shard_map/all_to_all | solution.py:171
  99.6 0.6 shard_map.76
  100.2 15.5 %all_to_all.16.shares = f32[8,8,256]{2,1,0:T(8,128)S(1)} all-to-all(f32[8,8,256]{2,1,0:T(8,128)S(1)} %shard_map.76), channel_id=1, replica_groups=mesh['ctx'=64,'head'=8] {'head'}, dimensions={0} | all-to-all | bytes 131072 | tf_op jit(solution)/shard_map/all_to_all | solution.py:176
  115.7 1.1 shard_map.77
  (8 shorter events, 0.0 us)
Async XLA Ops:
  0.0 40.4 %copy-start = (bf16[2048,256]{1,0:T(8,128)(2,1)S(1)}, bf16[2048,256]{1,0:T(8,128)(2,1)}, u32[]{:S(2)}) copy-start(bf16[2048,256]{1,0:T(8,128)(2,1)} %param.10) | copy-start | bytes 3145732
  32.9 7.2 %copy-start.5 = (s32[512]{0:T(512)S(1)}, s32[512]{0:T(512)}, u32[]{:S(2)}) copy-start(s32[512]{0:T(512)} %param.9) | copy-start | bytes 6148
  33.0 7.5 %copy-start.3 = (bf16[8,2048]{1,0:T(8,128)(2,1)S(1)}, bf16[8,2048]{1,0:T(8,128)(2,1)}, u32[]{:S(2)}) copy-start(bf16[8,2048]{1,0:T(8,128)(2,1)} %latents.1) | copy-start | bytes 98308
  33.0 39.8 %all-to-all-start = ((bf16[8,256,256]{2,1,0:T(8,128)(2,1)}), bf16[8,256,256]{2,1,0:T(8,128)(2,1)S(1)}, u32[]{:S(2)}, u32[]{:S(2)}) async-start(bf16[8,256,256]{2,1,0:T(8,128)(2,1)} %shard_map.73), calls=%async_computation | async-start | bytes 2097152 | tf_op jit(solution)/shard_map/all_to_all | solution.py:142
  40.1 32.7 %copy-start.2 = (bf16[2048,256]{1,0:T(8,128)(2,1)S(1)}, bf16[2048,256]{1,0:T(8,128)(2,1)}, u32[]{:S(2)}) copy-start(bf16[2048,256]{1,0:T(8,128)(2,1)} %wk.1) | copy-start | bytes 3145732
  74.7 24.9 %copy-start.1 = (bf16[256,2048]{1,0:T(8,128)(2,1)S(1)}, bf16[256,2048]{1,0:T(8,128)(2,1)}, u32[]{:S(2)}) copy-start(bf16[256,2048]{1,0:T(8,128)(2,1)} %w_out.1) | copy-start | bytes 3145732
  100.2 15.5 %copy-start.4 = (bf16[8,2048]{1,0:T(8,128)(2,1)S(1)}, bf16[8,2048]{1,0:T(8,128)(2,1)}, u32[]{:S(2)}) copy-start(bf16[8,2048]{1,0:T(8,128)(2,1)} %latents.1) | copy-start | bytes 98308

commit v5 on v4

--- a/solution.py
+++ b/solution.py
@@ -39,8 +39,11 @@
     return part[0] + (part[1] + part[2]), part[3] + (part[4] + part[5])
 
 
-def copies_kernel(context, out, sems):
-    copies = [pltpu.make_async_copy(context, out.at[d], sems.at[d]) for d in range(out.shape[0])]
+def copies_kernel(context, out, held, sem, sems):
+    fetch = pltpu.make_async_copy(context, held, sem)
+    fetch.start()
+    fetch.wait()
+    copies = [pltpu.make_async_copy(held, out.at[d], sems.at[d]) for d in range(out.shape[0])]
     for copy in copies:
         copy.start()
     for copy in copies:
@@ -137,7 +140,11 @@
         BF,
         [HBM],
         HBM,
-        [pltpu.SemaphoreType.DMA((heads_axis,))],
+        [
+            pltpu.VMEM(context.shape, BF),
+            pltpu.SemaphoreType.DMA,
+            pltpu.SemaphoreType.DMA((heads_axis,)),
+        ],
     )(pltpu.with_memory_space_constraint(context, pltpu.HBM))
     x = lax.all_to_all(copies, "head", 0, 0)
 

time: 117 us -> 86.4 us (0.74)
  Pallas kernels: 37.9 us -> 7.02 us
    pallas_call x1, Pallas kernels: 32.9 us -> 2.04 us  [on_device(): call(copies_kernel, (heads_axis,) + context.shape, BF, [HBM], HBM, [pltpu...]
where the time goes in v5:
time: 86.4 us; the launch traced here: 85.9 us
  blocking collectives  71 us (82%)
  starting transfers between devices  7.11 us (8%)
  Pallas kernels  7.02 us (8%)
    all_gather x5, blocking collectives, on_device(): q = lax.all_gather(q, 'ctx', axis=0, tiled=True, axis_index_groups=pairs)  32 us
    all_to_all x1, blocking collectives, on_device(): lax.all_to_all(part.reshape(chips, lat_dev, width + META), 'ctx', 0, 0, a...  21.3 us
    all_to_all x1, blocking collectives, on_device(): shares = lax.all_to_all(shares, 'head', 0, 0)  15.5 us
    all_to_all x1, starting transfers between devices, on_device(): x = lax.all_to_all(copies, 'head', 0, 0)  7.11 us
    all_gather x1, blocking collectives, on_device(): lax.all_gather(kv, 'ctx', axis=0, tiled=True, axis_index_groups=core_pairs)  2.31 us
    pallas_call x1, Pallas kernels, on_device(): call(copies_kernel, (heads_axis,) + context.shape, BF, [HBM], HBM, [pltpu...  2.04 us
    pallas_call x1, Pallas kernels, on_device(): call(key_value_kernel, (ctx_dev, 2 * width), BF, [VMEM, VMEM, HBM], VMEM,...  1.94 us
  transfers between devices with their start and end apart: 1, of which 0 were waited for; matrix products, arithmetic and copies ran while one was open for 1% of the time, Pallas kernels for 0%

profile of v5, /device:TPU:6, one launch (start us, length us, event | category | flops | bytes accessed | tf_op | source)
XLA Modules:
  0.0 85.9 jit_solution(16604539058247980705)
XLA Ops:
  0.0 0.0 copy-start
  0.0 2.0 %shard_map.73 = bf16[8,256,256]{2,1,0:T(8,128)(2,1)} custom-call(bf16[256,256]{1,0:T(8,128)(2,1)} %context.1), custom_call_target="tpu_custom_call" | custom-call | tf_op jit(solution)/shard_map/pallas_call | solution.py:137
  2.0 0.0 copy-start.5
  2.1 0.0 copy-start.3
  2.1 7.1 %all-to-all-start = ((bf16[8,256,256]{2,1,0:T(8,128)(2,1)}), bf16[8,256,256]{2,1,0:T(8,128)(2,1)S(1)}, u32[]{:S(2)}, u32[]{:S(2)}) async-start(bf16[8,256,256]{2,1,0:T(8,128)(2,1)} %shard_map.73), calls=%async_computation | async-start | bytes 2097152 | tf_op jit(solution)/shard_map/all_to_all | solution.py:149
  9.2 0.1 reshape.9
  9.4 0.1 reshape.12.lens
  9.5 0.0 copy-done
  9.6 0.2 fusion
  9.8 11.3 %all_gather.19 = bf16[16,256]{1,0:T(8,128)(2,1)S(1)} all-gather(bf16[8,256]{1,0:T(8,128)(2,1)S(1)} %fusion), channel_id=1, replica_groups={{0,256},{8,264},{16,272},{24,280},{32,288},{40,296},{48,304},{56,312},{..., dimensions={0}, use_global_device_ids=true | all-gather | bytes 12288 | tf_op jit(solution)/shard_map/all_gather | solution.py:158
  21.1 5.3 %all_gather.20 = bf16[32,256]{1,0:T(8,128)(2,1)S(1)} all-gather(bf16[16,256]{1,0:T(8,128)(2,1)S(1)} %all_gather.19), channel_id=1, replica_groups={{0,128},{8,136},{16,144},{24,152},{32,160},{40,168},{48,176},{56,184},{..., dimensions={0}, use_global_device_ids=true | all-gather | bytes 24576 | tf_op jit(solution)/shard_map/all_gather | solution.py:158
  26.3 5.9 %all_gather.21 = bf16[64,256]{1,0:T(8,128)(2,1)S(1)} all-gather(bf16[32,256]{1,0:T(8,128)(2,1)S(1)} %all_gather.20), channel_id=1, replica_groups={{0,32},{8,40},{16,48},{24,56},{64,96},{72,104},{80,112},{88,120},{128,1..., dimensions={0}, use_global_device_ids=true | all-gather | bytes 49152 | tf_op jit(solution)/shard_map/all_gather | solution.py:158
  32.3 4.6 %all_gather.22 = bf16[128,256]{1,0:T(8,128)(2,1)S(1)} all-gather(bf16[64,256]{1,0:T(8,128)(2,1)S(1)} %all_gather.21), channel_id=1, replica_groups={{0,64},{8,72},{16,80},{24,88},{32,96},{40,104},{48,112},{56,120},{128,1..., dimensions={0}, use_global_device_ids=true | all-gather | bytes 98304 | tf_op jit(solution)/shard_map/all_gather | solution.py:158
  36.8 4.9 %all_gather.23.q = bf16[256,256]{1,0:T(8,128)(2,1)S(1)} all-gather(bf16[128,256]{1,0:T(8,128)(2,1)S(1)} %all_gather.22), channel_id=1, replica_groups={{0,16},{8,24},{32,48},{40,56},{64,80},{72,88},{96,112},{104,120},{128,1..., dimensions={0}, use_global_device_ids=true | all-gather | bytes 196608 | tf_op jit(solution)/shard_map/all_gather | solution.py:158
  41.8 0.1 pad_add_fusion.place
  41.8 0.0 all-to-all-done.x
  41.8 1.9 %shard_map.74 = bf16[256,512]{1,0:T(8,128)(2,1)S(1)} custom-call(bf16[8,256,256]{2,1,0:T(8,128)(2,1)S(1)} %all-to-all-done.x, bf16[2048,256]{1,0:T(8,128)(2,1)S(1)} %copy-done.2, bf16[2048,256]{1,0:T(8,128)(2,1)} %wv_hbm.1), custom_call_target="tpu_custom_call" | custom-call | tf_op jit(solution)/shard_map/pallas_call | solution.py:166
  43.8 0.0 copy-start.1
  43.8 2.3 %all_gather.18.kv = bf16[512,512]{1,0:T(8,128)(2,1)S(1)} all-gather(bf16[256,512]{1,0:T(8,128)(2,1)S(1)} %shard_map.74), channel_id=1, replica_groups={{0,8},{16,24},{32,40},{48,56},{64,72},{80,88},{96,104},{112,120},{128,1..., dimensions={0}, use_global_device_ids=true | all-gather | bytes 786432 | tf_op jit(solution)/shard_map/all_gather | solution.py:174
  46.1 1.3 %shard_map.75 = bf16[256,384]{1,0:T(8,128)(2,1)S(1)} custom-call(s32[3]{0:T(128)S(1)} %pad_add_fusion.place, bf16[512,512]{1,0:T(8,128)(2,1)S(1)} %all_gather.18.kv, bf16[256,256]{1,0:T(8,128)(2,1)S(1)} %all_gather.23.q, s32[2,256,1]{2,1,0:T(8,128)S(1)} %reshape.12.lens), custom_call_target="tpu_custom_call" | custom-call | tf_op jit(solution)/shard_map/pallas_call | solution.py:175
  47.4 21.3 %all_to_all.15.got = bf16[32,8,384]{2,1,0:T(8,128)(2,1)S(1)} all-to-all(bf16[32,8,384]{2,1,0:T(8,128)(2,1)S(1)} %bitcast.7), channel_id=1, replica_groups={{0,256,128,384,32,288,160,416,64,320,192,448,96,352,224,480,16,272,144,..., dimensions={0} | all-to-all | bytes 393216 | tf_op jit(solution)/shard_map/all_to_all | solution.py:178
  68.7 0.6 shard_map.76
  69.3 15.5 %all_to_all.16.shares = f32[8,8,256]{2,1,0:T(8,128)S(1)} all-to-all(f32[8,8,256]{2,1,0:T(8,128)S(1)} %shard_map.76), channel_id=1, replica_groups=mesh['ctx'=64,'head'=8] {'head'}, dimensions={0} | all-to-all | bytes 131072 | tf_op jit(solution)/shard_map/all_to_all | solution.py:183
  84.8 1.1 %shard_map.77 = bf16[8,256]{1,0:T(8,128)(2,1)} custom-call(s32[3]{0:T(128)S(1)} %pad_add_fusion.place, f32[8,8,256]{2,1,0:T(8,128)S(1)} %all_to_all.16.shares, bf16[8,2048]{1,0:T(8,128)(2,1)S(1)} %copy-done.4), custom_call_target="tpu_custom_call" | custom-call | tf_op jit(solution)/shard_map/pallas_call | solution.py:184
  (8 shorter events, 0.0 us)
Async XLA Ops:
  0.0 9.5 %copy-start = (bf16[2048,256]{1,0:T(8,128)(2,1)S(1)}, bf16[2048,256]{1,0:T(8,128)(2,1)}, u32[]{:S(2)}) copy-start(bf16[2048,256]{1,0:T(8,128)(2,1)} %param.10) | copy-start | bytes 3145732
  2.0 7.2 %copy-start.5 = (s32[512]{0:T(512)S(1)}, s32[512]{0:T(512)}, u32[]{:S(2)}) copy-start(s32[512]{0:T(512)} %param.9) | copy-start | bytes 6148
  2.1 7.5 %copy-start.3 = (bf16[8,2048]{1,0:T(8,128)(2,1)S(1)}, bf16[8,2048]{1,0:T(8,128)(2,1)}, u32[]{:S(2)}) copy-start(bf16[8,2048]{1,0:T(8,128)(2,1)} %latents.1) | copy-start | bytes 98308
  2.1 39.8 %all-to-all-start = ((bf16[8,256,256]{2,1,0:T(8,128)(2,1)}), bf16[8,256,256]{2,1,0:T(8,128)(2,1)S(1)}, u32[]{:S(2)}, u32[]{:S(2)}) async-start(bf16[8,256,256]{2,1,0:T(8,128)(2,1)} %shard_map.73), calls=%async_computation | async-start | bytes 2097152 | tf_op jit(solution)/shard_map/all_to_all | solution.py:149
  9.2 32.7 %copy-start.2 = (bf16[2048,256]{1,0:T(8,128)(2,1)S(1)}, bf16[2048,256]{1,0:T(8,128)(2,1)}, u32[]{:S(2)}) copy-start(bf16[2048,256]{1,0:T(8,128)(2,1)} %wk.1) | copy-start | bytes 3145732
  43.8 24.9 %copy-start.1 = (bf16[256,2048]{1,0:T(8,128)(2,1)S(1)}, bf16[256,2048]{1,0:T(8,128)(2,1)}, u32[]{:S(2)}) copy-start(bf16[256,2048]{1,0:T(8,128)(2,1)} %w_out.1) | copy-start | bytes 3145732
  69.3 15.5 %copy-start.4 = (bf16[8,2048]{1,0:T(8,128)(2,1)S(1)}, bf16[8,2048]{1,0:T(8,128)(2,1)}, u32[]{:S(2)}) copy-start(bf16[8,2048]{1,0:T(8,128)(2,1)} %latents.1) | copy-start | bytes 98308

commit v6 on v4

v6 whole, which is shorter than its diff:
```python
import functools

import jax
import jax.numpy as jnp
from jax import lax
from jax.experimental import pallas as pl
from jax.experimental.pallas import tpu as pltpu
from jax.sharding import PartitionSpec as P

HD = 128
META = 128
CORES = 2
WV_PARTS = 2
COPY_PARTS = 2
MASKS = (24, 8, 4, 1, 3)
LAST_BIT = 2
BF = jnp.bfloat16
F32 = jnp.float32
LIMIT = 40 * 1024 * 1024


def split3(a):
    hi = a.astype(BF).astype(F32)
    rest = a - hi
    mid = rest.astype(BF).astype(F32)
    return [hi, mid, (rest - mid).astype(BF).astype(F32)]


def pack_meta(tops, totals):
    rows = tops[0].shape[0]
    lane = lax.broadcasted_iota(jnp.int32, (rows, META), 1)
    meta = jnp.zeros((rows, META), F32)
    column = 0
    for top, total in zip(tops, totals):
        for part in split3(top) + split3(total):
            meta = jnp.where(lane == column, part, meta)
            column += 1
    return meta.astype(BF)


def read_meta(meta, head):
    m = meta.astype(F32)
    part = [m[..., 6 * head + i : 6 * head + i + 1] for i in range(6)]
    return part[0] + (part[1] + part[2]), part[3] + (part[4] + part[5])


def copies_kernel(context, out, held, sems, out_sems):
    parts = sems.shape[0]
    step = held.shape[0] // parts
    rows = [pl.ds(i * step, step) for i in range(parts)]
    fetches = [
        pltpu.make_async_copy(context.at[r], held.at[r], sems.at[i]) for i, r in enumerate(rows)
    ]
    for fetch in fetches:
        fetch.start()
    sends = []
    for i, r in enumerate(rows):
        fetches[i].wait()
        for d in range(out.shape[0]):
            send = pltpu.make_async_copy(held.at[r], out.at[d, r], out_sems.at[i, d])
            send.start()
            sends.append(send)
    for send in sends:
        send.wait()


def key_value_kernel(x, wk, wv_hbm, out, wv, sems):
    width = wk.shape[1]
    step = wv.shape[0] // WV_PARTS
    parts = [pl.ds(i * step, step) for i in range(WV_PARTS)]
    fetches = [
        pltpu.make_async_copy(wv_hbm.at[part], wv.at[part], sems.at[i])
        for i, part in enumerate(parts)
    ]
    for fetch in fetches:
        fetch.start()
    feats = jnp.concatenate([x[f] for f in range(x.shape[0])], axis=1)
    out[:, :width] = jnp.dot(feats, wk[...], preferred_element_type=F32).astype(BF)
    for fetch in fetches:
        fetch.wait()
    out[:, width:] = jnp.dot(feats, wv[...], preferred_element_type=F32).astype(BF)


def attend_kernel(spots, bit, kv, q_own, q_got, lens, out):
    me = lax.axis_index("ctx")
    width = q_own.shape[1]
    positions = kv.shape[0]
    core, base = me % CORES, (me // CORES) * positions
    lower = (me // bit) % 2 == 0
    own, other = q_own[...], q_got[...]
    q = jnp.concatenate([jnp.where(lower, own, other), jnp.where(lower, other, own)], axis=0)
    rows = q.shape[0]
    step = rows // len(spots)
    natural = lens[core]
    last = jnp.concatenate([natural[p * step : (p + 1) * step] for p in spots], axis=0)
    visible = base + lax.broadcasted_iota(jnp.int32, (rows, positions), 1) < last
    ones = jnp.ones((positions, HD), BF)
    tops, totals = [], []
    for h in range(width // HD):
        cols = slice(h * HD, (h + 1) * HD)
        s = lax.dot_general(
            q[:, cols], kv[:, cols], (((1,), (1,)), ((), ())), preferred_element_type=F32
        )
        s = jnp.where(visible, s, -jnp.inf)
        top = jnp.maximum(jnp.max(s, axis=1, keepdims=True), -1e30)
        probs = jnp.exp(s - top).astype(BF)
        v = kv[:, width + h * HD : width + (h + 1) * HD]
        both = jnp.dot(probs, jnp.concatenate([v, ones], axis=1), preferred_element_type=F32)
        out[:, cols] = both[:, :HD].astype(BF)
        tops.append(top)
        totals.append(both[:, HD : HD + 1])
    out[:, width:] = pack_meta(tops, totals)


def project_kernel(got, w_out, latents, out):
    width = w_out.shape[0]
    parts = []
    for h in range(width // HD):
        top, total = read_meta(got[:, :, width:], h)
        scale = jnp.exp(top - jnp.max(top, axis=0, keepdims=True))
        o = jnp.sum(scale * got[:, :, h * HD : (h + 1) * HD].astype(F32), axis=0)
        parts.append((o / jnp.sum(scale * total, axis=0)).astype(BF))
    projected = jnp.dot(jnp.concatenate(parts, axis=1), w_out[...], preferred_element_type=F32)
    cols = out.shape[2]
    for d in range(out.shape[0]):
        out[d] = projected[:, d * cols : (d + 1) * cols]
    mine = lax.axis_index("head")
    first = pl.multiple_of(mine * cols, cols)
    out[mine] = out[mine] + latents[:, pl.ds(first, cols)].astype(F32)


def finish_kernel(shares, out):
    out[...] = jnp.sum(shares[...], axis=0).astype(BF)


VMEM = pl.BlockSpec(memory_space=pltpu.VMEM)
HBM = pl.BlockSpec(memory_space=pltpu.HBM)


def call(kernel, out_shape, in_specs, out_specs=VMEM, scratch=()):
    return pl.pallas_call(
        kernel,
        out_shape=out_shape,
        in_specs=in_specs,
        out_specs=out_specs,
        scratch_shapes=scratch,
        compiler_params=pltpu.CompilerParams(vmem_limit_bytes=LIMIT),
    )


def in_hbm(a):
    return pltpu.with_memory_space_constraint(a, pltpu.HBM)


def on_device(latents, context, lengths, w_query, w_key, w_value, w_out):
    lat_dev = latents.shape[0]
    groups = lax.axis_size("ctx")
    heads_axis = lax.axis_size("head")
    width = w_query.shape[1]
    ctx_dev = context.shape[0]
    chips = groups // CORES
    half = chips * lat_dev
    copies = call(
        copies_kernel,
        jax.ShapeDtypeStruct((heads_axis,) + context.shape, BF),
        [HBM],
        HBM,
        [
            pltpu.VMEM(context.shape, BF),
            pltpu.SemaphoreType.DMA((COPY_PARTS,)),
            pltpu.SemaphoreType.DMA((COPY_PARTS, heads_axis)),
        ],
    )(in_hbm(context))
    x = lax.all_to_all(copies, "head", 0, 0)

    qscale = 1.0 / HD**0.5
    q = (jnp.dot(latents, w_query, preferred_element_type=F32) * qscale).astype(BF)

    masks = [CORES * m for m in MASKS]
    held = [[i] for i in range(groups)]
    for step, mask in enumerate(masks):
        pairs = [
            [i, i ^ mask] for i in range(groups) if min(held[i]) < min(held[i ^ mask])
        ]
        if step < len(masks) - 1:
            q = lax.all_gather(q, "ctx", axis=0, tiled=True, axis_index_groups=pairs)
        for i, j in pairs:
            held[i] = held[j] = held[i] + held[j]
    q_got = lax.ppermute(q, "ctx", [(i, i ^ masks[-1]) for i in range(groups)])
    same_core = [held[c] for c in range(CORES)]
    spots = [d // CORES for d in held[0]]
    core_pairs = [[CORES * g + c for c in range(CORES)] for g in range(chips)]
    lens = lengths.reshape(chips, CORES, lat_dev).transpose(1, 0, 2).reshape(CORES, half, 1)

    kv = call(
        key_value_kernel,
        jax.ShapeDtypeStruct((ctx_dev, 2 * width), BF),
        [VMEM, VMEM, HBM],
        VMEM,
        [pltpu.VMEM(w_value.shape, BF), pltpu.SemaphoreType.DMA((WV_PARTS,))],
    )(x, w_key, in_hbm(w_value))
    kv = lax.all_gather(kv, "ctx", axis=0, tiled=True, axis_index_groups=core_pairs)
    part = call(
        functools.partial(attend_kernel, spots, CORES * LAST_BIT),
        jax.ShapeDtypeStruct((half, width + META), BF),
        [VMEM, VMEM, VMEM, VMEM],
    )(kv, q, q_got, lens)
    got = lax.all_to_all(
        part.reshape(chips, lat_dev, width + META), "ctx", 0, 0, axis_index_groups=same_core
    )
    cols_dev = w_out.shape[1] // heads_axis
    shares = call(
        project_kernel,
        jax.ShapeDtypeStruct((heads_axis, lat_dev, cols_dev), F32),
        [VMEM, VMEM, VMEM],
    )(got, w_out, latents)
    shares = lax.all_to_all(shares, "head", 0, 0)
    return call(finish_kernel, jax.ShapeDtypeStruct((lat_dev, cols_dev), BF), [VMEM])(shares)


def solution(mesh):
    in_specs = (
        P("ctx", None),
        P("ctx", "head"),
        P(),
        P(None, "head"),
        P(None, "head"),
        P(None, "head"),
        P("head", None),
    )
    return jax.shard_map(
        on_device, mesh=mesh, in_specs=in_specs, out_specs=P("ctx", "head"), check_vma=False
    )
```

time: 117 us -> 80.6 us (0.69)
  Pallas kernels: 37.9 us -> 6.8 us
  blocking collectives: 71 us -> 61.9 us
  starting transfers between devices: 7.11 us -> 9.49 us
    pallas_call x5, Pallas kernels: 37.9 us -> 6.8 us  [the longest x1 2.08 us: on_device(): call(copies_kernel, jax.ShapeDtypeStruct((heads_axis,) + context.shape, B...]
    all_gather x5 -> x4, blocking collectives: 32 us -> 25.8 us  [on_device(): q = lax.all_gather(q, 'ctx', axis=0, tiled=True, axis_index_groups=pairs)]
    all_to_all x1, blocking collectives: 15.5 us -> 10.8 us  [on_device(): shares = lax.all_to_all(shares, 'head', 0, 0)]
    ppermute x0 -> x1, starting transfers between devices: none -> 2.38 us  [on_device(): q_got = lax.ppermute(q, 'ctx', [(i, i ^ masks[-1]) for i in range(groups)])]
    all_to_all x1, blocking collectives: 21.3 us -> 23.1 us  [on_device(): lax.all_to_all(part.reshape(chips, lat_dev, width + META), 'ctx', 0, 0, a...]
  transfers between devices with their start and end apart: 1 -> 2, of which waited for: 0 -> 1; matrix products, arithmetic and copies ran while one was open for 1% -> 1% of each run, Pallas kernels for 0% -> 2%
where the time goes in v6:
time: 80.6 us; the launch traced here: 79.4 us
  blocking collectives  61.9 us (77%)
  starting transfers between devices  9.49 us (12%)
  Pallas kernels  6.8 us (8%)
    all_gather x4, blocking collectives, on_device(): q = lax.all_gather(q, 'ctx', axis=0, tiled=True, axis_index_groups=pairs)  25.8 us
    all_to_all x1, blocking collectives, on_device(): lax.all_to_all(part.reshape(chips, lat_dev, width + META), 'ctx', 0, 0, a...  23.1 us
    all_to_all x1, blocking collectives, on_device(): shares = lax.all_to_all(shares, 'head', 0, 0)  10.8 us
    all_to_all x1, starting transfers between devices, on_device(): x = lax.all_to_all(copies, 'head', 0, 0)  7.11 us
    ppermute x1, starting transfers between devices, on_device(): q_got = lax.ppermute(q, 'ctx', [(i, i ^ masks[-1]) for i in range(groups)])  2.38 us
    all_gather x1, blocking collectives, on_device(): lax.all_gather(kv, 'ctx', axis=0, tiled=True, axis_index_groups=core_pairs)  2.31 us
    pallas_call x1, Pallas kernels, on_device(): call(copies_kernel, jax.ShapeDtypeStruct((heads_axis,) + context.shape, B...  2.08 us
    pallas_call x1, Pallas kernels, on_device(): call(key_value_kernel, jax.ShapeDtypeStruct((ctx_dev, 2 * width), BF), [V...  1.92 us
  transfers between devices with their start and end apart: 2, of which 1 were waited for; matrix products, arithmetic and copies ran while one was open for 1% of the time, Pallas kernels for 2%

profile of v6, /device:TPU:6, one launch (start us, length us, event | category | flops | bytes accessed | tf_op | source)
XLA Modules:
  0.0 79.4 jit_solution(5992130854567109406)
XLA Ops:
  0.0 0.0 copy-start
  0.0 2.1 %shard_map.73 = bf16[8,256,256]{2,1,0:T(8,128)(2,1)} custom-call(bf16[256,256]{1,0:T(8,128)(2,1)} %context.1), custom_call_target="tpu_custom_call" | custom-call | tf_op jit(solution)/shard_map/pallas_call | solution.py:163
  2.1 0.0 copy-start.3
  2.1 7.1 %all-to-all-start = ((bf16[8,256,256]{2,1,0:T(8,128)(2,1)}), bf16[8,256,256]{2,1,0:T(8,128)(2,1)S(1)}, u32[]{:S(2)}, u32[]{:S(2)}) async-start(bf16[8,256,256]{2,1,0:T(8,128)(2,1)} %shard_map.73), calls=%async_computation | async-start | bytes 2097152 | tf_op jit(solution)/shard_map/all_to_all | solution.py:174
  9.2 0.0 copy-done
  9.2 0.0 copy-start.1
  9.2 0.2 fusion
  9.5 11.4 %all_gather.16 = bf16[16,256]{1,0:T(8,128)(2,1)S(1)} all-gather(bf16[8,256]{1,0:T(8,128)(2,1)S(1)} %fusion), channel_id=1, replica_groups={{0,384},{8,392},{16,400},{24,408},{32,416},{40,424},{48,432},{56,440},{..., dimensions={0}, use_global_device_ids=true | all-gather | bytes 12288 | tf_op jit(solution)/shard_map/all_gather | solution.py:186
  20.9 5.3 %all_gather.17 = bf16[32,256]{1,0:T(8,128)(2,1)S(1)} all-gather(bf16[16,256]{1,0:T(8,128)(2,1)S(1)} %all_gather.16), channel_id=1, replica_groups={{0,128},{8,136},{16,144},{24,152},{32,160},{40,168},{48,176},{56,184},{..., dimensions={0}, use_global_device_ids=true | all-gather | bytes 24576 | tf_op jit(solution)/shard_map/all_gather | solution.py:186
  26.2 4.4 %all_gather.18 = bf16[64,256]{1,0:T(8,128)(2,1)S(1)} all-gather(bf16[32,256]{1,0:T(8,128)(2,1)S(1)} %all_gather.17), channel_id=1, replica_groups={{0,64},{8,72},{16,80},{24,88},{32,96},{40,104},{48,112},{56,120},{128,1..., dimensions={0}, use_global_device_ids=true | all-gather | bytes 49152 | tf_op jit(solution)/shard_map/all_gather | solution.py:186
  30.6 4.7 %all_gather.19.q_own = bf16[128,256]{1,0:T(8,128)(2,1)S(1)} all-gather(bf16[64,256]{1,0:T(8,128)(2,1)S(1)} %all_gather.18), channel_id=1, replica_groups={{0,16},{8,24},{32,48},{40,56},{64,80},{72,88},{96,112},{104,120},{128,1..., dimensions={0}, use_global_device_ids=true | all-gather | bytes 98304 | tf_op jit(solution)/shard_map/all_gather | solution.py:186
  35.3 2.4 %collective-permute-start = (bf16[128,256]{1,0:T(8,128)(2,1)S(1)}, bf16[128,256]{1,0:T(8,128)(2,1)}, u32[]{:S(2)}, u32[]{:S(2)}) collective-permute-start(bf16[128,256]{1,0:T(8,128)(2,1)S(1)} %all_gather.19.q_own), channel_id=1, source_target_pairs={{0,48},{8,56},{16,32},{24,40},{32,16},{40,24},{48,0},{56,8},{64,11... | collective-permute-start | bytes 196616 | tf_op jit(solution)/shard_map/ppermute | solution.py:189
  37.7 0.1 reshape.9
  37.8 0.1 reshape.12.lens
  38.0 0.0 all-to-all-done.x
  38.0 1.9 %shard_map.74 = bf16[256,512]{1,0:T(8,128)(2,1)S(1)} custom-call(bf16[8,256,256]{2,1,0:T(8,128)(2,1)S(1)} %all-to-all-done.x, bf16[2048,256]{1,0:T(8,128)(2,1)S(1)} %copy-done.1, bf16[2048,256]{1,0:T(8,128)(2,1)} %wv_hbm.1), custom_call_target="tpu_custom_call" | custom-call | tf_op jit(solution)/shard_map/pallas_call | solution.py:195
  39.9 0.0 copy-start.2
  39.9 2.3 %all_gather.15.kv = bf16[512,512]{1,0:T(8,128)(2,1)S(1)} all-gather(bf16[256,512]{1,0:T(8,128)(2,1)S(1)} %shard_map.74), channel_id=1, replica_groups={{0,8},{16,24},{32,40},{48,56},{64,72},{80,88},{96,104},{112,120},{128,1..., dimensions={0}, use_global_device_ids=true | all-gather | bytes 786432 | tf_op jit(solution)/shard_map/all_gather | solution.py:202
  42.2 0.5 collective-permute-done.q_got
  42.8 1.6 %shard_map.75 = bf16[256,384]{1,0:T(8,128)(2,1)S(1)} custom-call(bf16[512,512]{1,0:T(8,128)(2,1)S(1)} %all_gather.15.kv, bf16[128,256]{1,0:T(8,128)(2,1)S(1)} %all_gather.19.q_own, bf16[128,256]{1,0:T(8,128)(2,1)} %collective-permute-done.q_got, s32[2,256,1]{2,1,0:T(8,128)S(1)} %reshape.12.lens), custom_call_target="tpu_custom_call" | custom-call | tf_op jit(solution)/shard_map/pallas_call | solution.py:203
  44.4 23.1 %all_to_all.15.got = bf16[32,8,384]{2,1,0:T(8,128)(2,1)S(1)} all-to-all(bf16[32,8,384]{2,1,0:T(8,128)(2,1)S(1)} %bitcast.4), channel_id=1, replica_groups={{0,384,128,256,64,448,192,320,16,400,144,272,80,464,208,336,32,416,160,..., dimensions={0} | all-to-all | bytes 393216 | tf_op jit(solution)/shard_map/all_to_all | solution.py:208
  67.5 0.6 shard_map.76
  68.0 10.8 %all_to_all.16.shares = f32[8,8,256]{2,1,0:T(8,128)S(1)} all-to-all(f32[8,8,256]{2,1,0:T(8,128)S(1)} %shard_map.76), channel_id=1, replica_groups=mesh['ctx'=64,'head'=8] {'head'}, dimensions={0} | all-to-all | bytes 131072 | tf_op jit(solution)/shard_map/all_to_all | solution.py:217
  78.8 0.6 shard_map.77
  (6 shorter events, 0.0 us)
Async XLA Ops:
  0.0 9.2 %copy-start = (bf16[2048,256]{1,0:T(8,128)(2,1)S(1)}, bf16[2048,256]{1,0:T(8,128)(2,1)}, u32[]{:S(2)}) copy-start(bf16[2048,256]{1,0:T(8,128)(2,1)} %param.10) | copy-start | bytes 3145732
  2.1 7.1 %copy-start.3 = (bf16[8,2048]{1,0:T(8,128)(2,1)S(1)}, bf16[8,2048]{1,0:T(8,128)(2,1)}, u32[]{:S(2)}) copy-start(bf16[8,2048]{1,0:T(8,128)(2,1)} %latents.1) | copy-start | bytes 98308
  2.1 35.9 %all-to-all-start = ((bf16[8,256,256]{2,1,0:T(8,128)(2,1)}), bf16[8,256,256]{2,1,0:T(8,128)(2,1)S(1)}, u32[]{:S(2)}, u32[]{:S(2)}) async-start(bf16[8,256,256]{2,1,0:T(8,128)(2,1)} %shard_map.73), calls=%async_computation | async-start | bytes 2097152 | tf_op jit(solution)/shard_map/all_to_all | solution.py:174
  9.2 28.7 %copy-start.1 = (bf16[2048,256]{1,0:T(8,128)(2,1)S(1)}, bf16[2048,256]{1,0:T(8,128)(2,1)}, u32[]{:S(2)}) copy-start(bf16[2048,256]{1,0:T(8,128)(2,1)} %wk.1) | copy-start | bytes 3145732
  30.6 7.1 %copy-start.4 = (s32[512]{0:T(512)S(1)}, s32[512]{0:T(512)}, u32[]{:S(2)}) copy-start(s32[512]{0:T(512)} %param.9) | copy-start | bytes 6148
  35.3 7.5 %collective-permute-start = (bf16[128,256]{1,0:T(8,128)(2,1)S(1)}, bf16[128,256]{1,0:T(8,128)(2,1)}, u32[]{:S(2)}, u32[]{:S(2)}) collective-permute-start(bf16[128,256]{1,0:T(8,128)(2,1)S(1)} %all_gather.19.q_own), channel_id=1, source_target_pairs={{0,48},{8,56},{16,32},{24,40},{32,16},{40,24},{48,0},{56,8},{64,11... | collective-permute-start | bytes 196616 | tf_op jit(solution)/shard_map/ppermute | solution.py:189
  39.9 27.5 %copy-start.2 = (bf16[256,2048]{1,0:T(8,128)(2,1)S(1)}, bf16[256,2048]{1,0:T(8,128)(2,1)}, u32[]{:S(2)}) copy-start(bf16[256,2048]{1,0:T(8,128)(2,1)} %w_out.1) | copy-start | bytes 3145732

commit v7 on v6

--- a/solution.py
+++ b/solution.py
@@ -91,8 +91,11 @@
     q = jnp.concatenate([jnp.where(lower, own, other), jnp.where(lower, other, own)], axis=0)
     rows = q.shape[0]
     step = rows // len(spots)
-    natural = lens[core]
-    last = jnp.concatenate([natural[p * step : (p + 1) * step] for p in spots], axis=0)
+    column = jnp.broadcast_to(lens[...].astype(F32), (8, lens.shape[1])).T[:, :1]
+    tiles = [column[i * step : (i + 1) * step] for i in range(CORES * len(spots))]
+    last = jnp.concatenate(
+        [jnp.where(core == 0, tiles[CORES * p], tiles[CORES * p + 1]) for p in spots], axis=0
+    ).astype(jnp.int32)
     visible = base + lax.broadcasted_iota(jnp.int32, (rows, positions), 1) < last
     ones = jnp.ones((positions, HD), BF)
     tops, totals = [], []
@@ -190,8 +193,6 @@
     same_core = [held[c] for c in range(CORES)]
     spots = [d // CORES for d in held[0]]
     core_pairs = [[CORES * g + c for c in range(CORES)] for g in range(chips)]
-    lens = lengths.reshape(chips, CORES, lat_dev).transpose(1, 0, 2).reshape(CORES, half, 1)
-
     kv = call(
         key_value_kernel,
         jax.ShapeDtypeStruct((ctx_dev, 2 * width), BF),
@@ -204,7 +205,7 @@
         functools.partial(attend_kernel, spots, CORES * LAST_BIT),
         jax.ShapeDtypeStruct((half, width + META), BF),
         [VMEM, VMEM, VMEM, VMEM],
-    )(kv, q, q_got, lens)
+    )(kv, q, q_got, lengths.reshape(1, -1))
     got = lax.all_to_all(
         part.reshape(chips, lat_dev, width + META), "ctx", 0, 0, axis_index_groups=same_core
     )

time: 80.6 us -> 79.7 us (0.989)
  Pallas kernels: 6.8 us -> 5.99 us
    pallas_call x1, Pallas kernels: 1.61 us -> 0.81 us  [on_device(): call(functools.partial(attend_kernel, spots, CORES * LAST_BIT), jax.Shape...]
  transfers between devices with their start and end apart: 2 -> 2, of which waited for: 1 -> 2; matrix products, arithmetic and copies ran while one was open for 1% -> 0% of each run, Pallas kernels for 2% -> 2%
where the time goes in v7:
time: 79.7 us; the launch traced here: 78.6 us
  blocking collectives  62 us (78%)
  starting transfers between devices  9.49 us (12%)
  Pallas kernels  5.99 us (8%)
    all_gather x4, blocking collectives, on_device(): q = lax.all_gather(q, 'ctx', axis=0, tiled=True, axis_index_groups=pairs)  25.7 us
    all_to_all x1, blocking collectives, on_device(): lax.all_to_all(part.reshape(chips, lat_dev, width + META), 'ctx', 0, 0, a...  23.3 us
    all_to_all x1, blocking collectives, on_device(): shares = lax.all_to_all(shares, 'head', 0, 0)  10.8 us
    all_to_all x1, starting transfers between devices, on_device(): x = lax.all_to_all(copies, 'head', 0, 0)  7.11 us
    ppermute x1, starting transfers between devices, on_device(): q_got = lax.ppermute(q, 'ctx', [(i, i ^ masks[-1]) for i in range(groups)])  2.37 us
    all_gather x1, blocking collectives, on_device(): lax.all_gather(kv, 'ctx', axis=0, tiled=True, axis_index_groups=core_pairs)  2.31 us
    pallas_call x1, Pallas kernels, on_device(): call(copies_kernel, jax.ShapeDtypeStruct((heads_axis,) + context.shape, B...  2.08 us
    pallas_call x1, Pallas kernels, on_device(): call(key_value_kernel, jax.ShapeDtypeStruct((ctx_dev, 2 * width), BF), [V...  1.92 us
  transfers between devices with their start and end apart: 2, of which 2 were waited for; matrix products, arithmetic and copies ran while one was open for 0% of the time, Pallas kernels for 2%

profile of v7, /device:TPU:6, one launch (start us, length us, event | category | flops | bytes accessed | tf_op | source)
XLA Modules:
  0.0 78.6 jit_solution(8211785419641743100)
XLA Ops:
  0.0 0.0 copy-start
  0.0 2.1 %shard_map.73 = bf16[8,256,256]{2,1,0:T(8,128)(2,1)} custom-call(bf16[256,256]{1,0:T(8,128)(2,1)} %context.1), custom_call_target="tpu_custom_call" | custom-call | tf_op jit(solution)/shard_map/pallas_call | solution.py:166
  2.1 0.0 copy-start.3
  2.1 7.1 %all-to-all-start = ((bf16[8,256,256]{2,1,0:T(8,128)(2,1)}), bf16[8,256,256]{2,1,0:T(8,128)(2,1)S(1)}, u32[]{:S(2)}, u32[]{:S(2)}) async-start(bf16[8,256,256]{2,1,0:T(8,128)(2,1)} %shard_map.73), calls=%async_computation | async-start | bytes 2097152 | tf_op jit(solution)/shard_map/all_to_all | solution.py:177
  9.2 0.0 copy-done
  9.2 0.0 copy-done.3
  9.2 0.0 copy-start.1
  9.2 0.2 fusion
  9.5 11.4 %all_gather.16 = bf16[16,256]{1,0:T(8,128)(2,1)S(1)} all-gather(bf16[8,256]{1,0:T(8,128)(2,1)S(1)} %fusion), channel_id=1, replica_groups={{0,384},{8,392},{16,400},{24,408},{32,416},{40,424},{48,432},{56,440},{..., dimensions={0}, use_global_device_ids=true | all-gather | bytes 12288 | tf_op jit(solution)/shard_map/all_gather | solution.py:189
  20.9 5.3 %all_gather.17 = bf16[32,256]{1,0:T(8,128)(2,1)S(1)} all-gather(bf16[16,256]{1,0:T(8,128)(2,1)S(1)} %all_gather.16), channel_id=1, replica_groups={{0,128},{8,136},{16,144},{24,152},{32,160},{40,168},{48,176},{56,184},{..., dimensions={0}, use_global_device_ids=true | all-gather | bytes 24576 | tf_op jit(solution)/shard_map/all_gather | solution.py:189
  26.2 4.4 %all_gather.18 = bf16[64,256]{1,0:T(8,128)(2,1)S(1)} all-gather(bf16[32,256]{1,0:T(8,128)(2,1)S(1)} %all_gather.17), channel_id=1, replica_groups={{0,64},{8,72},{16,80},{24,88},{32,96},{40,104},{48,112},{56,120},{128,1..., dimensions={0}, use_global_device_ids=true | all-gather | bytes 49152 | tf_op jit(solution)/shard_map/all_gather | solution.py:189
  30.6 4.6 %all_gather.19.q_own = bf16[128,256]{1,0:T(8,128)(2,1)S(1)} all-gather(bf16[64,256]{1,0:T(8,128)(2,1)S(1)} %all_gather.18), channel_id=1, replica_groups={{0,16},{8,24},{32,48},{40,56},{64,80},{72,88},{96,112},{104,120},{128,1..., dimensions={0}, use_global_device_ids=true | all-gather | bytes 98304 | tf_op jit(solution)/shard_map/all_gather | solution.py:189
  35.2 2.4 %collective-permute-start = (bf16[128,256]{1,0:T(8,128)(2,1)S(1)}, bf16[128,256]{1,0:T(8,128)(2,1)S(1)}, u32[]{:S(2)}, u32[]{:S(2)}) collective-permute-start(bf16[128,256]{1,0:T(8,128)(2,1)S(1)} %all_gather.19.q_own), channel_id=1, source_target_pairs={{0,48},{8,56},{16,32},{24,40},{32,16},{40,24},{48,0},{56,8},{64,11... | collective-permute-start | bytes 196616 | tf_op jit(solution)/shard_map/ppermute | solution.py:192
  37.6 0.4 all-to-all-done.x
  38.0 0.0 copy-done.1
  38.0 1.9 %shard_map.74 = bf16[256,512]{1,0:T(8,128)(2,1)S(1)} custom-call(bf16[8,256,256]{2,1,0:T(8,128)(2,1)S(1)} %all-to-all-done.x, bf16[2048,256]{1,0:T(8,128)(2,1)S(1)} %copy-done.1, bf16[2048,256]{1,0:T(8,128)(2,1)} %wv_hbm.1), custom_call_target="tpu_custom_call" | custom-call | tf_op jit(solution)/shard_map/pallas_call | solution.py:196
  39.9 0.0 copy-start.2
  39.9 2.3 %all_gather.15.kv = bf16[512,512]{1,0:T(8,128)(2,1)S(1)} all-gather(bf16[256,512]{1,0:T(8,128)(2,1)S(1)} %shard_map.74), channel_id=1, replica_groups={{0,8},{16,24},{32,40},{48,56},{64,72},{80,88},{96,104},{112,120},{128,1..., dimensions={0}, use_global_device_ids=true | all-gather | bytes 786432 | tf_op jit(solution)/shard_map/all_gather | solution.py:203
  42.2 0.3 collective-permute-done.q_got
  42.5 0.8 %shard_map.75 = bf16[256,384]{1,0:T(8,128)(2,1)S(1)} custom-call(bf16[512,512]{1,0:T(8,128)(2,1)S(1)} %all_gather.15.kv, bf16[128,256]{1,0:T(8,128)(2,1)S(1)} %all_gather.19.q_own, bf16[128,256]{1,0:T(8,128)(2,1)S(1)} %collective-permute-done.q_got, s32[1,512]{1,0:T(1,128)S(1)} %bitcast.5), custom_call_target="tpu_custom_call" | custom-call | tf_op jit(solution)/shard_map/pallas_call | solution.py:204
  43.4 23.3 %all_to_all.15.got = bf16[32,8,384]{2,1,0:T(8,128)(2,1)S(1)} all-to-all(bf16[32,8,384]{2,1,0:T(8,128)(2,1)S(1)} %bitcast.4), channel_id=1, replica_groups={{0,384,128,256,64,448,192,320,16,400,144,272,80,464,208,336,32,416,160,..., dimensions={0} | all-to-all | bytes 393216 | tf_op jit(solution)/shard_map/all_to_all | solution.py:209
  66.7 0.6 shard_map.76
  67.2 10.8 %all_to_all.16.shares = f32[8,8,256]{2,1,0:T(8,128)S(1)} all-to-all(f32[8,8,256]{2,1,0:T(8,128)S(1)} %shard_map.76), channel_id=1, replica_groups=mesh['ctx'=64,'head'=8] {'head'}, dimensions={0} | all-to-all | bytes 131072 | tf_op jit(solution)/shard_map/all_to_all | solution.py:218
  78.0 0.6 shard_map.77
  (3 shorter events, 0.0 us)
Async XLA Ops:
  0.0 9.2 %copy-start = (bf16[2048,256]{1,0:T(8,128)(2,1)S(1)}, bf16[2048,256]{1,0:T(8,128)(2,1)}, u32[]{:S(2)}) copy-start(bf16[2048,256]{1,0:T(8,128)(2,1)} %param.10) | copy-start | bytes 3145732
  2.1 7.1 %copy-start.3 = (bf16[8,2048]{1,0:T(8,128)(2,1)S(1)}, bf16[8,2048]{1,0:T(8,128)(2,1)}, u32[]{:S(2)}) copy-start(bf16[8,2048]{1,0:T(8,128)(2,1)} %latents.1) | copy-start | bytes 98308
  2.1 35.8 %all-to-all-start = ((bf16[8,256,256]{2,1,0:T(8,128)(2,1)}), bf16[8,256,256]{2,1,0:T(8,128)(2,1)S(1)}, u32[]{:S(2)}, u32[]{:S(2)}) async-start(bf16[8,256,256]{2,1,0:T(8,128)(2,1)} %shard_map.73), calls=%async_computation | async-start | bytes 2097152 | tf_op jit(solution)/shard_map/all_to_all | solution.py:177
  9.2 28.7 %copy-start.1 = (bf16[2048,256]{1,0:T(8,128)(2,1)S(1)}, bf16[2048,256]{1,0:T(8,128)(2,1)}, u32[]{:S(2)}) copy-start(bf16[2048,256]{1,0:T(8,128)(2,1)} %wk.1) | copy-start | bytes 3145732
  35.2 7.4 %collective-permute-start = (bf16[128,256]{1,0:T(8,128)(2,1)S(1)}, bf16[128,256]{1,0:T(8,128)(2,1)S(1)}, u32[]{:S(2)}, u32[]{:S(2)}) collective-permute-start(bf16[128,256]{1,0:T(8,128)(2,1)S(1)} %all_gather.19.q_own), channel_id=1, source_target_pairs={{0,48},{8,56},{16,32},{24,40},{32,16},{40,24},{48,0},{56,8},{64,11... | collective-permute-start | bytes 196616 | tf_op jit(solution)/shard_map/ppermute | solution.py:192
  38.0 4.6 %copy-start.4 = (s32[512]{0:T(512)S(1)}, s32[512]{0:T(512)}, u32[]{:S(2)}) copy-start(s32[512]{0:T(512)} %param.9) | copy-start | bytes 6148
  39.9 26.8 %copy-start.2 = (bf16[256,2048]{1,0:T(8,128)(2,1)S(1)}, bf16[256,2048]{1,0:T(8,128)(2,1)}, u32[]{:S(2)}) copy-start(bf16[256,2048]{1,0:T(8,128)(2,1)} %w_out.1) | copy-start | bytes 3145732

commit v8 on v7

--- a/solution.py
+++ b/solution.py
@@ -12,6 +12,7 @@
 CORES = 2
 WV_PARTS = 2
 COPY_PARTS = 2
+RING = (0, 1, 4, 5, 3, 2, 7, 6)
 MASKS = (24, 8, 4, 1, 3)
 LAST_BIT = 2
 BF = jnp.bfloat16
@@ -74,7 +75,7 @@
     ]
     for fetch in fetches:
         fetch.start()
-    feats = jnp.concatenate([x[f] for f in range(x.shape[0])], axis=1)
+    feats = jnp.concatenate([x[RING.index(f)] for f in range(x.shape[0])], axis=1)
     out[:, :width] = jnp.dot(feats, wk[...], preferred_element_type=F32).astype(BF)
     for fetch in fetches:
         fetch.wait()
@@ -125,10 +126,11 @@
         parts.append((o / jnp.sum(scale * total, axis=0)).astype(BF))
     projected = jnp.dot(jnp.concatenate(parts, axis=1), w_out[...], preferred_element_type=F32)
     cols = out.shape[2]
-    for d in range(out.shape[0]):
-        out[d] = projected[:, d * cols : (d + 1) * cols]
-    mine = lax.axis_index("head")
-    first = pl.multiple_of(mine * cols, cols)
+    for at, d in enumerate(RING):
+        out[at] = projected[:, d * cols : (d + 1) * cols]
+    head = lax.axis_index("head")
+    mine = sum(jnp.where(head == d, at, 0) for at, d in enumerate(RING))
+    first = pl.multiple_of(head * cols, cols)
     out[mine] = out[mine] + latents[:, pl.ds(first, cols)].astype(F32)
 
 
@@ -174,7 +176,7 @@
             pltpu.SemaphoreType.DMA((COPY_PARTS, heads_axis)),
         ],
     )(in_hbm(context))
-    x = lax.all_to_all(copies, "head", 0, 0)
+    x = lax.all_to_all(copies, "head", 0, 0, axis_index_groups=[RING])
 
     qscale = 1.0 / HD**0.5
     q = (jnp.dot(latents, w_query, preferred_element_type=F32) * qscale).astype(BF)
@@ -215,7 +217,7 @@
         jax.ShapeDtypeStruct((heads_axis, lat_dev, cols_dev), F32),
         [VMEM, VMEM, VMEM],
     )(got, w_out, latents)
-    shares = lax.all_to_all(shares, "head", 0, 0)
+    shares = lax.all_to_all(shares, "head", 0, 0, axis_index_groups=[RING])
     return call(finish_kernel, jax.ShapeDtypeStruct((lat_dev, cols_dev), BF), [VMEM])(shares)
 
 

time: 79.7 us -> 78.9 us (0.990)
  blocking collectives: 62 us -> 61.2 us
    all_to_all x1, blocking collectives: 23.3 us -> 20.9 us  [on_device(): lax.all_to_all(part.reshape(chips, lat_dev, width + META), 'ctx', 0, 0, a...]
    all_to_all x1, blocking collectives: 10.8 us -> 12.3 us  [on_device(): shares = lax.all_to_all(shares, 'head', 0, 0, axis_index_groups=[RING])]
  transfers between devices with their start and end apart: 2 -> 2, of which waited for: 2 -> 1; matrix products, arithmetic and copies ran while one was open for 0% -> 0% of each run, Pallas kernels for 2% -> 2%
where the time goes in v8:
time: 78.9 us; the launch traced here: 77.7 us
  blocking collectives  61.2 us (78%)
  starting transfers between devices  9.49 us (12%)
  Pallas kernels  5.99 us (8%)
    all_gather x4, blocking collectives, on_device(): q = lax.all_gather(q, 'ctx', axis=0, tiled=True, axis_index_groups=pairs)  25.7 us
    all_to_all x1, blocking collectives, on_device(): lax.all_to_all(part.reshape(chips, lat_dev, width + META), 'ctx', 0, 0, a...  20.9 us
    all_to_all x1, blocking collectives, on_device(): shares = lax.all_to_all(shares, 'head', 0, 0, axis_index_groups=[RING])  12.3 us
    all_to_all x1, starting transfers between devices, on_device(): x = lax.all_to_all(copies, 'head', 0, 0, axis_index_groups=[RING])  7.11 us
    ppermute x1, starting transfers between devices, on_device(): q_got = lax.ppermute(q, 'ctx', [(i, i ^ masks[-1]) for i in range(groups)])  2.37 us
    all_gather x1, blocking collectives, on_device(): lax.all_gather(kv, 'ctx', axis=0, tiled=True, axis_index_groups=core_pairs)  2.31 us
    pallas_call x1, Pallas kernels, on_device(): call(copies_kernel, jax.ShapeDtypeStruct((heads_axis,) + context.shape, B...  2.08 us
    pallas_call x1, Pallas kernels, on_device(): call(key_value_kernel, jax.ShapeDtypeStruct((ctx_dev, 2 * width), BF), [V...  1.92 us
  transfers between devices with their start and end apart: 2, of which 1 were waited for; matrix products, arithmetic and copies ran while one was open for 0% of the time, Pallas kernels for 2%

profile of v8, /device:TPU:6, one launch (start us, length us, event | category | flops | bytes accessed | tf_op | source)
XLA Modules:
  0.0 77.7 jit_solution(18200930668413068478)
XLA Ops:
  0.0 0.0 copy-start
  0.0 2.1 %shard_map.73 = bf16[8,256,256]{2,1,0:T(8,128)(2,1)} custom-call(bf16[256,256]{1,0:T(8,128)(2,1)} %context.1), custom_call_target="tpu_custom_call" | custom-call | tf_op jit(solution)/shard_map/pallas_call | solution.py:168
  2.1 0.0 copy-start.3
  2.1 7.1 %all-to-all-start = ((bf16[8,256,256]{2,1,0:T(8,128)(2,1)}), bf16[8,256,256]{2,1,0:T(8,128)(2,1)S(1)}, u32[]{:S(2)}, u32[]{:S(2)}) async-start(bf16[8,256,256]{2,1,0:T(8,128)(2,1)} %shard_map.73), calls=%async_computation | async-start | bytes 2097152 | tf_op jit(solution)/shard_map/all_to_all | solution.py:179
  9.2 0.0 copy-done
  9.2 0.0 copy-done.3
  9.2 0.0 copy-start.1
  9.2 0.2 fusion
  9.5 11.4 %all_gather.16 = bf16[16,256]{1,0:T(8,128)(2,1)S(1)} all-gather(bf16[8,256]{1,0:T(8,128)(2,1)S(1)} %fusion), channel_id=1, replica_groups={{0,384},{8,392},{16,400},{24,408},{32,416},{40,424},{48,432},{56,440},{..., dimensions={0}, use_global_device_ids=true | all-gather | bytes 12288 | tf_op jit(solution)/shard_map/all_gather | solution.py:191
  20.9 5.3 %all_gather.17 = bf16[32,256]{1,0:T(8,128)(2,1)S(1)} all-gather(bf16[16,256]{1,0:T(8,128)(2,1)S(1)} %all_gather.16), channel_id=1, replica_groups={{0,128},{8,136},{16,144},{24,152},{32,160},{40,168},{48,176},{56,184},{..., dimensions={0}, use_global_device_ids=true | all-gather | bytes 24576 | tf_op jit(solution)/shard_map/all_gather | solution.py:191
  26.2 4.4 %all_gather.18 = bf16[64,256]{1,0:T(8,128)(2,1)S(1)} all-gather(bf16[32,256]{1,0:T(8,128)(2,1)S(1)} %all_gather.17), channel_id=1, replica_groups={{0,64},{8,72},{16,80},{24,88},{32,96},{40,104},{48,112},{56,120},{128,1..., dimensions={0}, use_global_device_ids=true | all-gather | bytes 49152 | tf_op jit(solution)/shard_map/all_gather | solution.py:191
  30.6 4.6 %all_gather.19.q_own = bf16[128,256]{1,0:T(8,128)(2,1)S(1)} all-gather(bf16[64,256]{1,0:T(8,128)(2,1)S(1)} %all_gather.18), channel_id=1, replica_groups={{0,16},{8,24},{32,48},{40,56},{64,80},{72,88},{96,112},{104,120},{128,1..., dimensions={0}, use_global_device_ids=true | all-gather | bytes 98304 | tf_op jit(solution)/shard_map/all_gather | solution.py:191
  35.2 2.4 %collective-permute-start = (bf16[128,256]{1,0:T(8,128)(2,1)S(1)}, bf16[128,256]{1,0:T(8,128)(2,1)S(1)}, u32[]{:S(2)}, u32[]{:S(2)}) collective-permute-start(bf16[128,256]{1,0:T(8,128)(2,1)S(1)} %all_gather.19.q_own), channel_id=1, source_target_pairs={{0,48},{8,56},{16,32},{24,40},{32,16},{40,24},{48,0},{56,8},{64,11... | collective-permute-start | bytes 196616 | tf_op jit(solution)/shard_map/ppermute | solution.py:194
  37.6 0.0 all-to-all-done.x
  37.6 0.0 copy-start.4
  37.6 1.9 %shard_map.74 = bf16[256,512]{1,0:T(8,128)(2,1)S(1)} custom-call(bf16[8,256,256]{2,1,0:T(8,128)(2,1)S(1)} %all-to-all-done.x, bf16[2048,256]{1,0:T(8,128)(2,1)S(1)} %copy-done.1, bf16[2048,256]{1,0:T(8,128)(2,1)} %wv_hbm.1), custom_call_target="tpu_custom_call" | custom-call | tf_op jit(solution)/shard_map/pallas_call | solution.py:198
  39.5 0.0 copy-start.2
  39.5 2.3 %all_gather.15.kv = bf16[512,512]{1,0:T(8,128)(2,1)S(1)} all-gather(bf16[256,512]{1,0:T(8,128)(2,1)S(1)} %shard_map.74), channel_id=1, replica_groups={{0,8},{16,24},{32,40},{48,56},{64,72},{80,88},{96,104},{112,120},{128,1..., dimensions={0}, use_global_device_ids=true | all-gather | bytes 786432 | tf_op jit(solution)/shard_map/all_gather | solution.py:205
  41.8 0.7 collective-permute-done.q_got
  42.5 0.8 %shard_map.75 = bf16[256,384]{1,0:T(8,128)(2,1)S(1)} custom-call(bf16[512,512]{1,0:T(8,128)(2,1)S(1)} %all_gather.15.kv, bf16[128,256]{1,0:T(8,128)(2,1)S(1)} %all_gather.19.q_own, bf16[128,256]{1,0:T(8,128)(2,1)S(1)} %collective-permute-done.q_got, s32[1,512]{1,0:T(1,128)S(1)} %bitcast.5), custom_call_target="tpu_custom_call" | custom-call | tf_op jit(solution)/shard_map/pallas_call | solution.py:206
  43.4 20.9 %all_to_all.15.got = bf16[32,8,384]{2,1,0:T(8,128)(2,1)S(1)} all-to-all(bf16[32,8,384]{2,1,0:T(8,128)(2,1)S(1)} %bitcast.4), channel_id=1, replica_groups={{0,384,128,256,64,448,192,320,16,400,144,272,80,464,208,336,32,416,160,..., dimensions={0} | all-to-all | bytes 393216 | tf_op jit(solution)/shard_map/all_to_all | solution.py:211
  64.2 0.6 shard_map.76
  64.8 12.3 %all_to_all.16.shares = f32[8,8,256]{2,1,0:T(8,128)S(1)} all-to-all(f32[8,8,256]{2,1,0:T(8,128)S(1)} %shard_map.76), channel_id=1, replica_groups={{0,1,4,5,3,2,7,6},{8,9,12,13,11,10,15,14},{16,17,20,21,19,18,23,22},{24..., dimensions={0} | all-to-all | bytes 131072 | tf_op jit(solution)/shard_map/all_to_all | solution.py:220
  77.1 0.6 shard_map.77
  (3 shorter events, 0.0 us)
Async XLA Ops:
  0.0 9.2 %copy-start = (bf16[2048,256]{1,0:T(8,128)(2,1)S(1)}, bf16[2048,256]{1,0:T(8,128)(2,1)}, u32[]{:S(2)}) copy-start(bf16[2048,256]{1,0:T(8,128)(2,1)} %param.10) | copy-start | bytes 3145732
  2.1 7.1 %copy-start.3 = (bf16[8,2048]{1,0:T(8,128)(2,1)S(1)}, bf16[8,2048]{1,0:T(8,128)(2,1)}, u32[]{:S(2)}) copy-start(bf16[8,2048]{1,0:T(8,128)(2,1)} %latents.1) | copy-start | bytes 98308
  2.1 35.5 %all-to-all-start = ((bf16[8,256,256]{2,1,0:T(8,128)(2,1)}), bf16[8,256,256]{2,1,0:T(8,128)(2,1)S(1)}, u32[]{:S(2)}, u32[]{:S(2)}) async-start(bf16[8,256,256]{2,1,0:T(8,128)(2,1)} %shard_map.73), calls=%async_computation | async-start | bytes 2097152 | tf_op jit(solution)/shard_map/all_to_all | solution.py:179
  9.2 28.3 %copy-start.1 = (bf16[2048,256]{1,0:T(8,128)(2,1)S(1)}, bf16[2048,256]{1,0:T(8,128)(2,1)}, u32[]{:S(2)}) copy-start(bf16[2048,256]{1,0:T(8,128)(2,1)} %wk.1) | copy-start | bytes 3145732
  35.2 7.4 %collective-permute-start = (bf16[128,256]{1,0:T(8,128)(2,1)S(1)}, bf16[128,256]{1,0:T(8,128)(2,1)S(1)}, u32[]{:S(2)}, u32[]{:S(2)}) collective-permute-start(bf16[128,256]{1,0:T(8,128)(2,1)S(1)} %all_gather.19.q_own), channel_id=1, source_target_pairs={{0,48},{8,56},{16,32},{24,40},{32,16},{40,24},{48,0},{56,8},{64,11... | collective-permute-start | bytes 196616 | tf_op jit(solution)/shard_map/ppermute | solution.py:194
  37.6 5.0 %copy-start.4 = (s32[512]{0:T(512)S(1)}, s32[512]{0:T(512)}, u32[]{:S(2)}) copy-start(s32[512]{0:T(512)} %param.9) | copy-start | bytes 6148
  39.5 24.7 %copy-start.2 = (bf16[256,2048]{1,0:T(8,128)(2,1)S(1)}, bf16[256,2048]{1,0:T(8,128)(2,1)}, u32[]{:S(2)}) copy-start(bf16[256,2048]{1,0:T(8,128)(2,1)} %w_out.1) | copy-start | bytes 3145732

commit v9 on v8

--- a/solution.py
+++ b/solution.py
@@ -13,7 +13,7 @@
 WV_PARTS = 2
 COPY_PARTS = 2
 RING = (0, 1, 4, 5, 3, 2, 7, 6)
-MASKS = (24, 8, 4, 1, 3)
+MASKS = (8, 4, 24, 1, 3)
 LAST_BIT = 2
 BF = jnp.bfloat16
 F32 = jnp.float32

time: 78.9 us -> 78.1 us (0.990)
  blocking collectives: 61.2 us -> 60.3 us
    all_to_all x1, blocking collectives: 20.9 us -> 20 us  [on_device(): lax.all_to_all(part.reshape(chips, lat_dev, width + META), 'ctx', 0, 0, a...]
where the time goes in v9:
time: 78.1 us; the launch traced here: 76.9 us
  blocking collectives  60.3 us (77%)
  starting transfers between devices  9.49 us (12%)
  Pallas kernels  5.99 us (8%)
    all_gather x4, blocking collectives, on_device(): q = lax.all_gather(q, 'ctx', axis=0, tiled=True, axis_index_groups=pairs)  25.7 us
    all_to_all x1, blocking collectives, on_device(): lax.all_to_all(part.reshape(chips, lat_dev, width + META), 'ctx', 0, 0, a...  20 us
    all_to_all x1, blocking collectives, on_device(): shares = lax.all_to_all(shares, 'head', 0, 0, axis_index_groups=[RING])  12.3 us
    all_to_all x1, starting transfers between devices, on_device(): x = lax.all_to_all(copies, 'head', 0, 0, axis_index_groups=[RING])  7.11 us
    ppermute x1, starting transfers between devices, on_device(): q_got = lax.ppermute(q, 'ctx', [(i, i ^ masks[-1]) for i in range(groups)])  2.37 us
    all_gather x1, blocking collectives, on_device(): lax.all_gather(kv, 'ctx', axis=0, tiled=True, axis_index_groups=core_pairs)  2.31 us
    pallas_call x1, Pallas kernels, on_device(): call(copies_kernel, jax.ShapeDtypeStruct((heads_axis,) + context.shape, B...  2.08 us
    pallas_call x1, Pallas kernels, on_device(): call(key_value_kernel, jax.ShapeDtypeStruct((ctx_dev, 2 * width), BF), [V...  1.92 us
  transfers between devices with their start and end apart: 2, of which 1 were waited for; matrix products, arithmetic and copies ran while one was open for 0% of the time, Pallas kernels for 2%

profile of v9, /device:TPU:6, one launch (start us, length us, event | category | flops | bytes accessed | tf_op | source)
XLA Modules:
  0.0 76.9 jit_solution(9614001694465711610)
XLA Ops:
  0.0 0.0 copy-start
  0.0 2.1 %shard_map.73 = bf16[8,256,256]{2,1,0:T(8,128)(2,1)} custom-call(bf16[256,256]{1,0:T(8,128)(2,1)} %context.1), custom_call_target="tpu_custom_call" | custom-call | tf_op jit(solution)/shard_map/pallas_call | solution.py:168
  2.1 0.0 copy-start.3
  2.1 7.1 %all-to-all-start = ((bf16[8,256,256]{2,1,0:T(8,128)(2,1)}), bf16[8,256,256]{2,1,0:T(8,128)(2,1)S(1)}, u32[]{:S(2)}, u32[]{:S(2)}) async-start(bf16[8,256,256]{2,1,0:T(8,128)(2,1)} %shard_map.73), calls=%async_computation | async-start | bytes 2097152 | tf_op jit(solution)/shard_map/all_to_all | solution.py:179
  9.2 0.0 copy-done
  9.2 0.0 copy-done.3
  9.2 0.0 copy-start.1
  9.2 0.2 fusion
  9.5 6.6 %all_gather.16 = bf16[16,256]{1,0:T(8,128)(2,1)S(1)} all-gather(bf16[8,256]{1,0:T(8,128)(2,1)S(1)} %fusion), channel_id=1, replica_groups={{0,128},{8,136},{16,144},{24,152},{32,160},{40,168},{48,176},{56,184},{..., dimensions={0}, use_global_device_ids=true | all-gather | bytes 12288 | tf_op jit(solution)/shard_map/all_gather | solution.py:191
  16.1 4.7 %all_gather.17 = bf16[32,256]{1,0:T(8,128)(2,1)S(1)} all-gather(bf16[16,256]{1,0:T(8,128)(2,1)S(1)} %all_gather.16), channel_id=1, replica_groups={{0,64},{8,72},{16,80},{24,88},{32,96},{40,104},{48,112},{56,120},{128,1..., dimensions={0}, use_global_device_ids=true | all-gather | bytes 24576 | tf_op jit(solution)/shard_map/all_gather | solution.py:191
  20.8 9.8 %all_gather.18 = bf16[64,256]{1,0:T(8,128)(2,1)S(1)} all-gather(bf16[32,256]{1,0:T(8,128)(2,1)S(1)} %all_gather.17), channel_id=1, replica_groups={{0,384},{8,392},{16,400},{24,408},{32,416},{40,424},{48,432},{56,440},{..., dimensions={0}, use_global_device_ids=true | all-gather | bytes 49152 | tf_op jit(solution)/shard_map/all_gather | solution.py:191
  30.6 4.6 %all_gather.19.q_own = bf16[128,256]{1,0:T(8,128)(2,1)S(1)} all-gather(bf16[64,256]{1,0:T(8,128)(2,1)S(1)} %all_gather.18), channel_id=1, replica_groups={{0,16},{8,24},{32,48},{40,56},{64,80},{72,88},{96,112},{104,120},{128,1..., dimensions={0}, use_global_device_ids=true | all-gather | bytes 98304 | tf_op jit(solution)/shard_map/all_gather | solution.py:191
  35.2 2.4 %collective-permute-start = (bf16[128,256]{1,0:T(8,128)(2,1)S(1)}, bf16[128,256]{1,0:T(8,128)(2,1)S(1)}, u32[]{:S(2)}, u32[]{:S(2)}) collective-permute-start(bf16[128,256]{1,0:T(8,128)(2,1)S(1)} %all_gather.19.q_own), channel_id=1, source_target_pairs={{0,48},{8,56},{16,32},{24,40},{32,16},{40,24},{48,0},{56,8},{64,11... | collective-permute-start | bytes 196616 | tf_op jit(solution)/shard_map/ppermute | solution.py:194
  37.6 0.0 all-to-all-done.x
  37.6 0.0 copy-start.4
  37.6 1.9 %shard_map.74 = bf16[256,512]{1,0:T(8,128)(2,1)S(1)} custom-call(bf16[8,256,256]{2,1,0:T(8,128)(2,1)S(1)} %all-to-all-done.x, bf16[2048,256]{1,0:T(8,128)(2,1)S(1)} %copy-done.1, bf16[2048,256]{1,0:T(8,128)(2,1)} %wv_hbm.1), custom_call_target="tpu_custom_call" | custom-call | tf_op jit(solution)/shard_map/pallas_call | solution.py:198
  39.5 0.0 copy-start.2
  39.5 2.3 %all_gather.15.kv = bf16[512,512]{1,0:T(8,128)(2,1)S(1)} all-gather(bf16[256,512]{1,0:T(8,128)(2,1)S(1)} %shard_map.74), channel_id=1, replica_groups={{0,8},{16,24},{32,40},{48,56},{64,72},{80,88},{96,104},{112,120},{128,1..., dimensions={0}, use_global_device_ids=true | all-gather | bytes 786432 | tf_op jit(solution)/shard_map/all_gather | solution.py:205
  41.9 0.7 collective-permute-done.q_got
  42.5 0.8 %shard_map.75 = bf16[256,384]{1,0:T(8,128)(2,1)S(1)} custom-call(bf16[512,512]{1,0:T(8,128)(2,1)S(1)} %all_gather.15.kv, bf16[128,256]{1,0:T(8,128)(2,1)S(1)} %all_gather.19.q_own, bf16[128,256]{1,0:T(8,128)(2,1)S(1)} %collective-permute-done.q_got, s32[1,512]{1,0:T(1,128)S(1)} %bitcast.5), custom_call_target="tpu_custom_call" | custom-call | tf_op jit(solution)/shard_map/pallas_call | solution.py:206
  43.4 20.0 %all_to_all.15.got = bf16[32,8,384]{2,1,0:T(8,128)(2,1)S(1)} all-to-all(bf16[32,8,384]{2,1,0:T(8,128)(2,1)S(1)} %bitcast.4), channel_id=1, replica_groups={{0,128,64,192,256,384,320,448,16,144,80,208,272,400,336,464,32,160,96,2..., dimensions={0} | all-to-all | bytes 393216 | tf_op jit(solution)/shard_map/all_to_all | solution.py:211
  63.4 0.6 shard_map.76
  64.0 12.3 %all_to_all.16.shares = f32[8,8,256]{2,1,0:T(8,128)S(1)} all-to-all(f32[8,8,256]{2,1,0:T(8,128)S(1)} %shard_map.76), channel_id=1, replica_groups={{0,1,4,5,3,2,7,6},{8,9,12,13,11,10,15,14},{16,17,20,21,19,18,23,22},{24..., dimensions={0} | all-to-all | bytes 131072 | tf_op jit(solution)/shard_map/all_to_all | solution.py:220
  76.3 0.6 shard_map.77
  (3 shorter events, 0.0 us)
Async XLA Ops:
  0.0 9.2 %copy-start = (bf16[2048,256]{1,0:T(8,128)(2,1)S(1)}, bf16[2048,256]{1,0:T(8,128)(2,1)}, u32[]{:S(2)}) copy-start(bf16[2048,256]{1,0:T(8,128)(2,1)} %param.10) | copy-start | bytes 3145732
  2.1 7.1 %copy-start.3 = (bf16[8,2048]{1,0:T(8,128)(2,1)S(1)}, bf16[8,2048]{1,0:T(8,128)(2,1)}, u32[]{:S(2)}) copy-start(bf16[8,2048]{1,0:T(8,128)(2,1)} %latents.1) | copy-start | bytes 98308
  2.1 35.5 %all-to-all-start = ((bf16[8,256,256]{2,1,0:T(8,128)(2,1)}), bf16[8,256,256]{2,1,0:T(8,128)(2,1)S(1)}, u32[]{:S(2)}, u32[]{:S(2)}) async-start(bf16[8,256,256]{2,1,0:T(8,128)(2,1)} %shard_map.73), calls=%async_computation | async-start | bytes 2097152 | tf_op jit(solution)/shard_map/all_to_all | solution.py:179
  9.2 28.3 %copy-start.1 = (bf16[2048,256]{1,0:T(8,128)(2,1)S(1)}, bf16[2048,256]{1,0:T(8,128)(2,1)}, u32[]{:S(2)}) copy-start(bf16[2048,256]{1,0:T(8,128)(2,1)} %wk.1) | copy-start | bytes 3145732
  35.2 7.4 %collective-permute-start = (bf16[128,256]{1,0:T(8,128)(2,1)S(1)}, bf16[128,256]{1,0:T(8,128)(2,1)S(1)}, u32[]{:S(2)}, u32[]{:S(2)}) collective-permute-start(bf16[128,256]{1,0:T(8,128)(2,1)S(1)} %all_gather.19.q_own), channel_id=1, source_target_pairs={{0,48},{8,56},{16,32},{24,40},{32,16},{40,24},{48,0},{56,8},{64,11... | collective-permute-start | bytes 196616 | tf_op jit(solution)/shard_map/ppermute | solution.py:194
  37.6 5.0 %copy-start.4 = (s32[512]{0:T(512)S(1)}, s32[512]{0:T(512)}, u32[]{:S(2)}) copy-start(s32[512]{0:T(512)} %param.9) | copy-start | bytes 6148
  39.5 23.9 %copy-start.2 = (bf16[256,2048]{1,0:T(8,128)(2,1)S(1)}, bf16[256,2048]{1,0:T(8,128)(2,1)}, u32[]{:S(2)}) copy-start(bf16[256,2048]{1,0:T(8,128)(2,1)} %w_out.1) | copy-start | bytes 3145732

commit v10 on v9

--- a/solution.py
+++ b/solution.py
@@ -116,7 +116,7 @@
     out[:, width:] = pack_meta(tops, totals)
 
 
-def project_kernel(got, w_out, latents, out):
+def project_kernel(got, w_out, out):
     width = w_out.shape[0]
     parts = []
     for h in range(width // HD):
@@ -127,15 +127,14 @@
     projected = jnp.dot(jnp.concatenate(parts, axis=1), w_out[...], preferred_element_type=F32)
     cols = out.shape[2]
     for at, d in enumerate(RING):
-        out[at] = projected[:, d * cols : (d + 1) * cols]
-    head = lax.axis_index("head")
-    mine = sum(jnp.where(head == d, at, 0) for at, d in enumerate(RING))
-    first = pl.multiple_of(head * cols, cols)
-    out[mine] = out[mine] + latents[:, pl.ds(first, cols)].astype(F32)
-
-
-def finish_kernel(shares, out):
-    out[...] = jnp.sum(shares[...], axis=0).astype(BF)
+        out[at] = projected[:, d * cols : (d + 1) * cols].astype(BF)
+
+
+def finish_kernel(shares, latents, out):
+    cols = out.shape[1]
+    first = pl.multiple_of(lax.axis_index("head") * cols, cols)
+    summed = jnp.sum(shares[...].astype(F32), axis=0)
+    out[...] = (latents[:, pl.ds(first, cols)].astype(F32) + summed).astype(BF)
 
 
 VMEM = pl.BlockSpec(memory_space=pltpu.VMEM)
@@ -214,11 +213,13 @@
     cols_dev = w_out.shape[1] // heads_axis
     shares = call(
         project_kernel,
-        jax.ShapeDtypeStruct((heads_axis, lat_dev, cols_dev), F32),
-        [VMEM, VMEM, VMEM],
-    )(got, w_out, latents)
+        jax.ShapeDtypeStruct((heads_axis, lat_dev, cols_dev), BF),
+        [VMEM, VMEM],
+    )(got, w_out)
     shares = lax.all_to_all(shares, "head", 0, 0, axis_index_groups=[RING])
-    return call(finish_kernel, jax.ShapeDtypeStruct((lat_dev, cols_dev), BF), [VMEM])(shares)
+    return call(
+        finish_kernel, jax.ShapeDtypeStruct((lat_dev, cols_dev), BF), [VMEM, VMEM]
+    )(shares, latents)
 
 
 def solution(mesh):

time: 78.1 us -> 77.9 us (level)
  no operation moved by 1% of the time
where the time goes in v10:
time: 77.9 us; the launch traced here: 76.8 us
  blocking collectives  60.2 us (77%)
  starting transfers between devices  9.49 us (12%)
  Pallas kernels  5.99 us (8%)
    all_gather x4, blocking collectives, on_device(): q = lax.all_gather(q, 'ctx', axis=0, tiled=True, axis_index_groups=pairs)  25.7 us
    all_to_all x1, blocking collectives, on_device(): lax.all_to_all(part.reshape(chips, lat_dev, width + META), 'ctx', 0, 0, a...  20 us
    all_to_all x1, blocking collectives, on_device(): shares = lax.all_to_all(shares, 'head', 0, 0, axis_index_groups=[RING])  12.2 us
    all_to_all x1, starting transfers between devices, on_device(): x = lax.all_to_all(copies, 'head', 0, 0, axis_index_groups=[RING])  7.11 us
    ppermute x1, starting transfers between devices, on_device(): q_got = lax.ppermute(q, 'ctx', [(i, i ^ masks[-1]) for i in range(groups)])  2.37 us
    all_gather x1, blocking collectives, on_device(): lax.all_gather(kv, 'ctx', axis=0, tiled=True, axis_index_groups=core_pairs)  2.31 us
    pallas_call x1, Pallas kernels, on_device(): call(copies_kernel, jax.ShapeDtypeStruct((heads_axis,) + context.shape, B...  2.08 us
    pallas_call x1, Pallas kernels, on_device(): call(key_value_kernel, jax.ShapeDtypeStruct((ctx_dev, 2 * width), BF), [V...  1.92 us
  transfers between devices with their start and end apart: 2, of which 1 were waited for; matrix products, arithmetic and copies ran while one was open for 0% of the time, Pallas kernels for 2%

profile of v10, /device:TPU:6, one launch (start us, length us, event | category | flops | bytes accessed | tf_op | source)
XLA Modules:
  0.0 76.8 jit_solution(8358857609813551930)
XLA Ops:
  0.0 0.0 copy-start
  0.0 2.1 %shard_map.73 = bf16[8,256,256]{2,1,0:T(8,128)(2,1)} custom-call(bf16[256,256]{1,0:T(8,128)(2,1)} %context.1), custom_call_target="tpu_custom_call" | custom-call | tf_op jit(solution)/shard_map/pallas_call | solution.py:167
  2.1 0.0 copy-start.3
  2.1 7.1 %all-to-all-start = ((bf16[8,256,256]{2,1,0:T(8,128)(2,1)}), bf16[8,256,256]{2,1,0:T(8,128)(2,1)S(1)}, u32[]{:S(2)}, u32[]{:S(2)}) async-start(bf16[8,256,256]{2,1,0:T(8,128)(2,1)} %shard_map.73), calls=%async_computation | async-start | bytes 2097152 | tf_op jit(solution)/shard_map/all_to_all | solution.py:178
  9.2 0.0 copy-done
  9.2 0.0 copy-start.2
  9.2 0.2 fusion
  9.5 6.6 %all_gather.16 = bf16[16,256]{1,0:T(8,128)(2,1)S(1)} all-gather(bf16[8,256]{1,0:T(8,128)(2,1)S(1)} %fusion), channel_id=1, replica_groups={{0,128},{8,136},{16,144},{24,152},{32,160},{40,168},{48,176},{56,184},{..., dimensions={0}, use_global_device_ids=true | all-gather | bytes 12288 | tf_op jit(solution)/shard_map/all_gather | solution.py:190
  16.1 4.7 %all_gather.17 = bf16[32,256]{1,0:T(8,128)(2,1)S(1)} all-gather(bf16[16,256]{1,0:T(8,128)(2,1)S(1)} %all_gather.16), channel_id=1, replica_groups={{0,64},{8,72},{16,80},{24,88},{32,96},{40,104},{48,112},{56,120},{128,1..., dimensions={0}, use_global_device_ids=true | all-gather | bytes 24576 | tf_op jit(solution)/shard_map/all_gather | solution.py:190
  20.8 9.8 %all_gather.18 = bf16[64,256]{1,0:T(8,128)(2,1)S(1)} all-gather(bf16[32,256]{1,0:T(8,128)(2,1)S(1)} %all_gather.17), channel_id=1, replica_groups={{0,384},{8,392},{16,400},{24,408},{32,416},{40,424},{48,432},{56,440},{..., dimensions={0}, use_global_device_ids=true | all-gather | bytes 49152 | tf_op jit(solution)/shard_map/all_gather | solution.py:190
  30.6 4.6 %all_gather.19.q_own = bf16[128,256]{1,0:T(8,128)(2,1)S(1)} all-gather(bf16[64,256]{1,0:T(8,128)(2,1)S(1)} %all_gather.18), channel_id=1, replica_groups={{0,16},{8,24},{32,48},{40,56},{64,80},{72,88},{96,112},{104,120},{128,1..., dimensions={0}, use_global_device_ids=true | all-gather | bytes 98304 | tf_op jit(solution)/shard_map/all_gather | solution.py:190
  35.2 2.4 %collective-permute-start = (bf16[128,256]{1,0:T(8,128)(2,1)S(1)}, bf16[128,256]{1,0:T(8,128)(2,1)S(1)}, u32[]{:S(2)}, u32[]{:S(2)}) collective-permute-start(bf16[128,256]{1,0:T(8,128)(2,1)S(1)} %all_gather.19.q_own), channel_id=1, source_target_pairs={{0,48},{8,56},{16,32},{24,40},{32,16},{40,24},{48,0},{56,8},{64,11... | collective-permute-start | bytes 196616 | tf_op jit(solution)/shard_map/ppermute | solution.py:193
  37.6 0.0 all-to-all-done.x
  37.6 0.0 copy-done.2
  37.6 0.0 copy-start.4
  37.6 1.9 %shard_map.74 = bf16[256,512]{1,0:T(8,128)(2,1)S(1)} custom-call(bf16[8,256,256]{2,1,0:T(8,128)(2,1)S(1)} %all-to-all-done.x, bf16[2048,256]{1,0:T(8,128)(2,1)S(1)} %copy-done.2, bf16[2048,256]{1,0:T(8,128)(2,1)} %wv_hbm.1), custom_call_target="tpu_custom_call" | custom-call | tf_op jit(solution)/shard_map/pallas_call | solution.py:197
  39.5 0.0 copy-start.1
  39.5 2.3 %all_gather.15.kv = bf16[512,512]{1,0:T(8,128)(2,1)S(1)} all-gather(bf16[256,512]{1,0:T(8,128)(2,1)S(1)} %shard_map.74), channel_id=1, replica_groups={{0,8},{16,24},{32,40},{48,56},{64,72},{80,88},{96,104},{112,120},{128,1..., dimensions={0}, use_global_device_ids=true | all-gather | bytes 786432 | tf_op jit(solution)/shard_map/all_gather | solution.py:204
  41.9 0.7 collective-permute-done.q_got
  42.5 0.8 %shard_map.75 = bf16[256,384]{1,0:T(8,128)(2,1)S(1)} custom-call(bf16[512,512]{1,0:T(8,128)(2,1)S(1)} %all_gather.15.kv, bf16[128,256]{1,0:T(8,128)(2,1)S(1)} %all_gather.19.q_own, bf16[128,256]{1,0:T(8,128)(2,1)S(1)} %collective-permute-done.q_got, s32[1,512]{1,0:T(1,128)S(1)} %bitcast.5), custom_call_target="tpu_custom_call" | custom-call | tf_op jit(solution)/shard_map/pallas_call | solution.py:205
  43.4 20.0 %all_to_all.15.got = bf16[32,8,384]{2,1,0:T(8,128)(2,1)S(1)} all-to-all(bf16[32,8,384]{2,1,0:T(8,128)(2,1)S(1)} %bitcast.4), channel_id=1, replica_groups={{0,128,64,192,256,384,320,448,16,144,80,208,272,400,336,464,32,160,96,2..., dimensions={0} | all-to-all | bytes 393216 | tf_op jit(solution)/shard_map/all_to_all | solution.py:210
  63.4 0.6 shard_map.76
  64.0 12.2 %all_to_all.16.shares = bf16[8,8,256]{2,1,0:T(8,128)(2,1)S(1)} all-to-all(bf16[8,8,256]{2,1,0:T(8,128)(2,1)S(1)} %shard_map.76), channel_id=1, replica_groups={{0,1,4,5,3,2,7,6},{8,9,12,13,11,10,15,14},{16,17,20,21,19,18,23,22},{24..., dimensions={0} | all-to-all | bytes 65536 | tf_op jit(solution)/shard_map/all_to_all | solution.py:219
  76.1 0.6 shard_map.77
  (3 shorter events, 0.0 us)
Async XLA Ops:
  0.0 9.2 %copy-start = (bf16[2048,256]{1,0:T(8,128)(2,1)S(1)}, bf16[2048,256]{1,0:T(8,128)(2,1)}, u32[]{:S(2)}) copy-start(bf16[2048,256]{1,0:T(8,128)(2,1)} %param.10) | copy-start | bytes 3145732
  2.1 7.1 %copy-start.3 = (bf16[8,2048]{1,0:T(8,128)(2,1)S(1)}, bf16[8,2048]{1,0:T(8,128)(2,1)}, u32[]{:S(2)}) copy-start(bf16[8,2048]{1,0:T(8,128)(2,1)} %latents.1) | copy-start | bytes 98308
  2.1 35.5 %all-to-all-start = ((bf16[8,256,256]{2,1,0:T(8,128)(2,1)}), bf16[8,256,256]{2,1,0:T(8,128)(2,1)S(1)}, u32[]{:S(2)}, u32[]{:S(2)}) async-start(bf16[8,256,256]{2,1,0:T(8,128)(2,1)} %shard_map.73), calls=%async_computation | async-start | bytes 2097152 | tf_op jit(solution)/shard_map/all_to_all | solution.py:178
  9.2 28.3 %copy-start.2 = (bf16[2048,256]{1,0:T(8,128)(2,1)S(1)}, bf16[2048,256]{1,0:T(8,128)(2,1)}, u32[]{:S(2)}) copy-start(bf16[2048,256]{1,0:T(8,128)(2,1)} %wk.1) | copy-start | bytes 3145732
  35.2 7.4 %collective-permute-start = (bf16[128,256]{1,0:T(8,128)(2,1)S(1)}, bf16[128,256]{1,0:T(8,128)(2,1)S(1)}, u32[]{:S(2)}, u32[]{:S(2)}) collective-permute-start(bf16[128,256]{1,0:T(8,128)(2,1)S(1)} %all_gather.19.q_own), channel_id=1, source_target_pairs={{0,48},{8,56},{16,32},{24,40},{32,16},{40,24},{48,0},{56,8},{64,11... | collective-permute-start | bytes 196616 | tf_op jit(solution)/shard_map/ppermute | solution.py:193
  37.6 5.0 %copy-start.4 = (s32[512]{0:T(512)S(1)}, s32[512]{0:T(512)}, u32[]{:S(2)}) copy-start(s32[512]{0:T(512)} %param.9) | copy-start | bytes 6148
  39.5 23.9 %copy-start.1 = (bf16[256,2048]{1,0:T(8,128)(2,1)S(1)}, bf16[256,2048]{1,0:T(8,128)(2,1)}, u32[]{:S(2)}) copy-start(bf16[256,2048]{1,0:T(8,128)(2,1)} %w_out.1) | copy-start | bytes 3145732

commit v11 on v10

--- a/solution.py
+++ b/solution.py
@@ -10,8 +10,8 @@
 HD = 128
 META = 128
 CORES = 2
-WV_PARTS = 2
-COPY_PARTS = 2
+WV_PARTS = 1
+COPY_PARTS = 1
 RING = (0, 1, 4, 5, 3, 2, 7, 6)
 MASKS = (8, 4, 24, 1, 3)
 LAST_BIT = 2

time: 77.9 us -> 77.8 us (level)
  transfers between devices with their start and end apart: 2 -> 2, of which waited for: 1 -> 1; matrix products, arithmetic and copies ran while one was open for 0% -> 0% of each run, Pallas kernels for 2% -> 3%
where the time goes in v11:
time: 77.8 us; the launch traced here: 76.7 us
  blocking collectives  60.2 us (77%)
  starting transfers between devices  9.49 us (12%)
  Pallas kernels  5.96 us (8%)
    all_gather x4, blocking collectives, on_device(): q = lax.all_gather(q, 'ctx', axis=0, tiled=True, axis_index_groups=pairs)  25.7 us
    all_to_all x1, blocking collectives, on_device(): lax.all_to_all(part.reshape(chips, lat_dev, width + META), 'ctx', 0, 0, a...  20 us
    all_to_all x1, blocking collectives, on_device(): shares = lax.all_to_all(shares, 'head', 0, 0, axis_index_groups=[RING])  12.2 us
    all_to_all x1, starting transfers between devices, on_device(): x = lax.all_to_all(copies, 'head', 0, 0, axis_index_groups=[RING])  7.11 us
    ppermute x1, starting transfers between devices, on_device(): q_got = lax.ppermute(q, 'ctx', [(i, i ^ masks[-1]) for i in range(groups)])  2.37 us
    all_gather x1, blocking collectives, on_device(): lax.all_gather(kv, 'ctx', axis=0, tiled=True, axis_index_groups=core_pairs)  2.31 us
    pallas_call x1, Pallas kernels, on_device(): call(copies_kernel, jax.ShapeDtypeStruct((heads_axis,) + context.shape, B...  2.04 us
    pallas_call x1, Pallas kernels, on_device(): call(key_value_kernel, jax.ShapeDtypeStruct((ctx_dev, 2 * width), BF), [V...  1.94 us
  transfers between devices with their start and end apart: 2, of which 1 were waited for; matrix products, arithmetic and copies ran while one was open for 0% of the time, Pallas kernels for 3%

profile of v11, /device:TPU:6, one launch (start us, length us, event | category | flops | bytes accessed | tf_op | source)
XLA Modules:
  0.0 76.7 jit_solution(9696121461091113585)
XLA Ops:
  0.0 0.0 copy-start
  0.0 2.0 %shard_map.73 = bf16[8,256,256]{2,1,0:T(8,128)(2,1)} custom-call(bf16[256,256]{1,0:T(8,128)(2,1)} %context.1), custom_call_target="tpu_custom_call" | custom-call | tf_op jit(solution)/shard_map/pallas_call | solution.py:167
  2.0 0.0 copy-start.3
  2.1 7.1 %all-to-all-start = ((bf16[8,256,256]{2,1,0:T(8,128)(2,1)}), bf16[8,256,256]{2,1,0:T(8,128)(2,1)S(1)}, u32[]{:S(2)}, u32[]{:S(2)}) async-start(bf16[8,256,256]{2,1,0:T(8,128)(2,1)} %shard_map.73), calls=%async_computation | async-start | bytes 2097152 | tf_op jit(solution)/shard_map/all_to_all | solution.py:178
  9.2 0.0 copy-done.3
  9.2 0.0 copy-start.2
  9.2 0.2 fusion
  9.4 6.6 %all_gather.16 = bf16[16,256]{1,0:T(8,128)(2,1)S(1)} all-gather(bf16[8,256]{1,0:T(8,128)(2,1)S(1)} %fusion), channel_id=1, replica_groups={{0,128},{8,136},{16,144},{24,152},{32,160},{40,168},{48,176},{56,184},{..., dimensions={0}, use_global_device_ids=true | all-gather | bytes 12288 | tf_op jit(solution)/shard_map/all_gather | solution.py:190
  16.0 4.7 %all_gather.17 = bf16[32,256]{1,0:T(8,128)(2,1)S(1)} all-gather(bf16[16,256]{1,0:T(8,128)(2,1)S(1)} %all_gather.16), channel_id=1, replica_groups={{0,64},{8,72},{16,80},{24,88},{32,96},{40,104},{48,112},{56,120},{128,1..., dimensions={0}, use_global_device_ids=true | all-gather | bytes 24576 | tf_op jit(solution)/shard_map/all_gather | solution.py:190
  20.7 9.8 %all_gather.18 = bf16[64,256]{1,0:T(8,128)(2,1)S(1)} all-gather(bf16[32,256]{1,0:T(8,128)(2,1)S(1)} %all_gather.17), channel_id=1, replica_groups={{0,384},{8,392},{16,400},{24,408},{32,416},{40,424},{48,432},{56,440},{..., dimensions={0}, use_global_device_ids=true | all-gather | bytes 49152 | tf_op jit(solution)/shard_map/all_gather | solution.py:190
  30.6 4.6 %all_gather.19.q_own = bf16[128,256]{1,0:T(8,128)(2,1)S(1)} all-gather(bf16[64,256]{1,0:T(8,128)(2,1)S(1)} %all_gather.18), channel_id=1, replica_groups={{0,16},{8,24},{32,48},{40,56},{64,80},{72,88},{96,112},{104,120},{128,1..., dimensions={0}, use_global_device_ids=true | all-gather | bytes 98304 | tf_op jit(solution)/shard_map/all_gather | solution.py:190
  35.1 2.4 %collective-permute-start = (bf16[128,256]{1,0:T(8,128)(2,1)S(1)}, bf16[128,256]{1,0:T(8,128)(2,1)S(1)}, u32[]{:S(2)}, u32[]{:S(2)}) collective-permute-start(bf16[128,256]{1,0:T(8,128)(2,1)S(1)} %all_gather.19.q_own), channel_id=1, source_target_pairs={{0,48},{8,56},{16,32},{24,40},{32,16},{40,24},{48,0},{56,8},{64,11... | collective-permute-start | bytes 196616 | tf_op jit(solution)/shard_map/ppermute | solution.py:193
  37.5 0.0 all-to-all-done.x
  37.5 0.0 copy-done.2
  37.5 0.0 copy-start.4
  37.6 1.9 %shard_map.74 = bf16[256,512]{1,0:T(8,128)(2,1)S(1)} custom-call(bf16[8,256,256]{2,1,0:T(8,128)(2,1)S(1)} %all-to-all-done.x, bf16[2048,256]{1,0:T(8,128)(2,1)S(1)} %copy-done.2, bf16[2048,256]{1,0:T(8,128)(2,1)} %wv_hbm.1), custom_call_target="tpu_custom_call" | custom-call | tf_op jit(solution)/shard_map/pallas_call | solution.py:197
  39.5 0.0 copy-start.1
  39.5 2.3 %all_gather.15.kv = bf16[512,512]{1,0:T(8,128)(2,1)S(1)} all-gather(bf16[256,512]{1,0:T(8,128)(2,1)S(1)} %shard_map.74), channel_id=1, replica_groups={{0,8},{16,24},{32,40},{48,56},{64,72},{80,88},{96,104},{112,120},{128,1..., dimensions={0}, use_global_device_ids=true | all-gather | bytes 786432 | tf_op jit(solution)/shard_map/all_gather | solution.py:204
  41.8 0.7 collective-permute-done.q_got
  42.5 0.8 %shard_map.75 = bf16[256,384]{1,0:T(8,128)(2,1)S(1)} custom-call(bf16[512,512]{1,0:T(8,128)(2,1)S(1)} %all_gather.15.kv, bf16[128,256]{1,0:T(8,128)(2,1)S(1)} %all_gather.19.q_own, bf16[128,256]{1,0:T(8,128)(2,1)S(1)} %collective-permute-done.q_got, s32[1,512]{1,0:T(1,128)S(1)} %bitcast.5), custom_call_target="tpu_custom_call" | custom-call | tf_op jit(solution)/shard_map/pallas_call | solution.py:205
  43.3 20.0 %all_to_all.15.got = bf16[32,8,384]{2,1,0:T(8,128)(2,1)S(1)} all-to-all(bf16[32,8,384]{2,1,0:T(8,128)(2,1)S(1)} %bitcast.4), channel_id=1, replica_groups={{0,128,64,192,256,384,320,448,16,144,80,208,272,400,336,464,32,160,96,2..., dimensions={0} | all-to-all | bytes 393216 | tf_op jit(solution)/shard_map/all_to_all | solution.py:210
  63.4 0.6 shard_map.76
  63.9 12.2 %all_to_all.16.shares = bf16[8,8,256]{2,1,0:T(8,128)(2,1)S(1)} all-to-all(bf16[8,8,256]{2,1,0:T(8,128)(2,1)S(1)} %shard_map.76), channel_id=1, replica_groups={{0,1,4,5,3,2,7,6},{8,9,12,13,11,10,15,14},{16,17,20,21,19,18,23,22},{24..., dimensions={0} | all-to-all | bytes 65536 | tf_op jit(solution)/shard_map/all_to_all | solution.py:219
  76.1 0.6 shard_map.77
  (3 shorter events, 0.0 us)
Async XLA Ops:
  0.0 9.2 %copy-start = (bf16[2048,256]{1,0:T(8,128)(2,1)S(1)}, bf16[2048,256]{1,0:T(8,128)(2,1)}, u32[]{:S(2)}) copy-start(bf16[2048,256]{1,0:T(8,128)(2,1)} %param.10) | copy-start | bytes 3145732
  2.0 7.1 %copy-start.3 = (bf16[8,2048]{1,0:T(8,128)(2,1)S(1)}, bf16[8,2048]{1,0:T(8,128)(2,1)}, u32[]{:S(2)}) copy-start(bf16[8,2048]{1,0:T(8,128)(2,1)} %latents.1) | copy-start | bytes 98308
  2.1 35.5 %all-to-all-start = ((bf16[8,256,256]{2,1,0:T(8,128)(2,1)}), bf16[8,256,256]{2,1,0:T(8,128)(2,1)S(1)}, u32[]{:S(2)}, u32[]{:S(2)}) async-start(bf16[8,256,256]{2,1,0:T(8,128)(2,1)} %shard_map.73), calls=%async_computation | async-start | bytes 2097152 | tf_op jit(solution)/shard_map/all_to_all | solution.py:178
  9.2 28.3 %copy-start.2 = (bf16[2048,256]{1,0:T(8,128)(2,1)S(1)}, bf16[2048,256]{1,0:T(8,128)(2,1)}, u32[]{:S(2)}) copy-start(bf16[2048,256]{1,0:T(8,128)(2,1)} %wk.1) | copy-start | bytes 3145732
  35.1 7.4 %collective-permute-start = (bf16[128,256]{1,0:T(8,128)(2,1)S(1)}, bf16[128,256]{1,0:T(8,128)(2,1)S(1)}, u32[]{:S(2)}, u32[]{:S(2)}) collective-permute-start(bf16[128,256]{1,0:T(8,128)(2,1)S(1)} %all_gather.19.q_own), channel_id=1, source_target_pairs={{0,48},{8,56},{16,32},{24,40},{32,16},{40,24},{48,0},{56,8},{64,11... | collective-permute-start | bytes 196616 | tf_op jit(solution)/shard_map/ppermute | solution.py:193
  37.5 5.0 %copy-start.4 = (s32[512]{0:T(512)S(1)}, s32[512]{0:T(512)}, u32[]{:S(2)}) copy-start(s32[512]{0:T(512)} %param.9) | copy-start | bytes 6148
  39.5 23.9 %copy-start.1 = (bf16[256,2048]{1,0:T(8,128)(2,1)S(1)}, bf16[256,2048]{1,0:T(8,128)(2,1)}, u32[]{:S(2)}) copy-start(bf16[256,2048]{1,0:T(8,128)(2,1)} %w_out.1) | copy-start | bytes 3145732
